TPU v7x, 512 devices: a whole 4x4x16 slice. The times are simulated.
512 devices in a mesh: seq: 16 (over z_lo, core), chan: 32 (over z_hi, y, x).
Axes of the slice: x: 4, y: 4, z: 16 (z_hi: 2, z_lo: 8; z = z_hi * 8 + z_lo), core: 2. Of those that a mesh axis runs over, the one named last changes fastest.
Arguments:
- features: bfloat16 [3, 16384, 8192], P(None, ('seq', 'chan')), may hold values from -6 to 6
- short_weights: float32 [3, 3, 8192], replicated, may hold values from -3.5 to 3.5
- doc_lengths: int32 [64], replicated, may hold values from 1 to 2048, 16384 in all
- residues: float32 [16, 8192], P(None, 'chan'), may hold values from -1.5 to 1.5
- rates: float32 [16, 8192], P(None, 'chan'), may hold values from 3.0517578e-05 to 0.05
- skip: float32 [8192], P('chan'), may hold values from -4 to 4
Outputs:
- mixed: bfloat16 [16384, 8192], P(('seq', 'chan'))
Inputs may be any that keep to these rules, and one draw needn't show every extreme that they name: `doc_lengths`: the lengths sum to 16384 and the largest is exactly 2048.
All inputs are finite; a program needn't handle non-finite values.
Results may differ from a plain program's by a relative error of at most 0.01.
Values may be sent and summed in bfloat16 or wider, within the bound.
A program may use at most 64 MiB of HBM per device.

v0:
```python
import math

import jax
import jax.numpy as jnp
from jax import lax
from jax.sharding import PartitionSpec as P

TAPS = 3


def passed_along(x, axis, by):
    peers = lax.axis_size(axis)
    pairs = [(i, i + by) for i in range(peers) if 0 <= i + by < peers]
    return lax.ppermute(x, axis, pairs)


def matmul_form(form, table, data):
    return jnp.einsum(
        form, table, data, precision=lax.Precision.HIGHEST, preferred_element_type=jnp.float32
    )


def angle_table(rows, cols, modulus):
    turns = rows[:, None] * cols[None, :] % modulus
    angle = turns.astype(jnp.float32) * (2.0 * math.pi / modulus)
    return (jnp.cos(angle), jnp.sin(angle))


def featurize(tokens, rim, short_weights, doc_lengths, first):
    count = tokens.shape[1]
    extended = jnp.concatenate([rim, tokens], axis=1).astype(jnp.float32)
    position = first + jnp.arange(count, dtype=jnp.int32)
    starts = jnp.cumsum(doc_lengths) - doc_lengths
    begin = jnp.max(jnp.where(starts[None, :] <= position[:, None], starts[None, :], 0), axis=1)
    streams = jnp.zeros(tokens.shape, jnp.float32)
    for offset in range(TAPS):
        valid = (position - offset >= begin).astype(jnp.float32)
        window = extended[:, TAPS - 1 - offset : TAPS - 1 - offset + count, :]
        streams = streams + valid[None, :, None] * short_weights[:, offset, None, :] * window
    return streams


def spectrum_of(freq, residues, rates, length):
    total = 2 * length
    half = freq.astype(jnp.float32) * (math.pi / total)
    shape = (1,) + freq.shape + (1,)
    sine = jnp.sin(half).reshape(shape)
    cosine = jnp.cos(half).reshape(shape)
    parity = (1 - 2 * (freq % 2)).astype(jnp.float32).reshape(shape)
    wide = (rates.shape[0],) + (1,) * freq.ndim + (rates.shape[1],)
    rate = rates.reshape(wide)
    residue = residues.reshape(wide)
    decay = jnp.exp(-rate)
    gap = -jnp.expm1(-rate)
    gain = residue * jnp.sqrt(-jnp.expm1(-2.0 * rate))
    tail = jnp.exp(-rate * length)
    numer = 1.0 - parity * tail
    den_re = gap + 2.0 * decay * sine * sine
    den_im = 2.0 * decay * sine * cosine
    scale = gain * numer / (den_re * den_re + den_im * den_im)
    return (jnp.sum(scale * den_re, axis=0), -jnp.sum(scale * den_im, axis=0))


def row_tables(outer, inner):
    count = outer * inner
    outer_ids = jnp.arange(outer, dtype=jnp.int32)
    inner_ids = jnp.arange(inner, dtype=jnp.int32)
    cos_outer, sin_outer = angle_table(outer_ids, outer_ids, outer)
    cos_twist, sin_twist = angle_table(outer_ids, inner_ids, count)
    cos_inner, sin_inner = angle_table(inner_ids, inner_ids, inner)
    return (
        cos_outer,
        sin_outer,
        cos_twist[None, :, :, None],
        sin_twist[None, :, :, None],
        cos_inner,
        sin_inner,
    )


def forward_rows(real, imag):
    lead, count, chans = real.shape
    inner = math.gcd(count, 128)
    outer = count // inner
    cos_outer, sin_outer, cos_twist, sin_twist, cos_inner, sin_inner = row_tables(outer, inner)
    real = real.reshape(lead, outer, inner, chans)
    imag = imag.reshape(lead, outer, inner, chans)
    real, imag = (
        matmul_form("ub,lbmh->lumh", cos_outer, real)
        + matmul_form("ub,lbmh->lumh", sin_outer, imag),
        matmul_form("ub,lbmh->lumh", cos_outer, imag)
        - matmul_form("ub,lbmh->lumh", sin_outer, real),
    )
    real, imag = (real * cos_twist + imag * sin_twist, imag * cos_twist - real * sin_twist)
    real, imag = (
        matmul_form("vm,lumh->luvh", cos_inner, real)
        + matmul_form("vm,lumh->luvh", sin_inner, imag),
        matmul_form("vm,lumh->luvh", cos_inner, imag)
        - matmul_form("vm,lumh->luvh", sin_inner, real),
    )
    return (real, imag)


def inverse_rows(real, imag):
    lead, outer, inner, chans = real.shape
    cos_outer, sin_outer, cos_twist, sin_twist, cos_inner, sin_inner = row_tables(outer, inner)
    real, imag = (
        matmul_form("vm,luvh->lumh", cos_inner, real)
        - matmul_form("vm,luvh->lumh", sin_inner, imag),
        matmul_form("vm,luvh->lumh", cos_inner, imag)
        + matmul_form("vm,luvh->lumh", sin_inner, real),
    )
    real, imag = (real * cos_twist - imag * sin_twist, imag * cos_twist + real * sin_twist)
    real, imag = (
        matmul_form("ub,lumh->lbmh", cos_outer, real)
        - matmul_form("ub,lumh->lbmh", sin_outer, imag),
        matmul_form("ub,lumh->lbmh", cos_outer, imag)
        + matmul_form("ub,lumh->lbmh", sin_outer, real),
    )
    return (real.reshape(lead, outer * inner, chans), imag.reshape(lead, outer * inner, chans))


def spectral(real, imag, owned, pairs, residues, rates, length):
    real, imag = forward_rows(real, imag)
    outer, inner = (real.shape[1], real.shape[2])
    slots = (
        jnp.arange(outer, dtype=jnp.int32)[:, None]
        + outer * jnp.arange(inner, dtype=jnp.int32)[None, :]
    )
    freq = owned[:, None, None] + pairs * slots[None, :, :]
    spec_re, spec_im = spectrum_of(freq, residues, rates, length)
    real, imag = (real * spec_re - imag * spec_im, real * spec_im + imag * spec_re)
    return inverse_rows(real, imag)


def blocks_forward(values, offsets, pairs, total):
    count = values.shape[0]
    cos_a, sin_a = angle_table(
        jnp.arange(pairs, dtype=jnp.int32), jnp.arange(count, dtype=jnp.int32), pairs
    )
    real = matmul_form("ca,ash->csh", cos_a, values)
    imag = -matmul_form("ca,ash->csh", sin_a, values)
    cos_t, sin_t = angle_table(jnp.arange(pairs, dtype=jnp.int32), offsets, total)
    cos_t = cos_t[:, :, None]
    sin_t = sin_t[:, :, None]
    return (real * cos_t + imag * sin_t, imag * cos_t - real * sin_t)


def blocks_inverse(real, imag, offsets, count, total):
    pairs = real.shape[0]
    cos_t, sin_t = angle_table(jnp.arange(pairs, dtype=jnp.int32), offsets, total)
    cos_t = cos_t[:, :, None]
    sin_t = sin_t[:, :, None]
    real, imag = (real * cos_t - imag * sin_t, imag * cos_t + real * sin_t)
    cos_a, sin_a = angle_table(
        jnp.arange(pairs, dtype=jnp.int32), jnp.arange(count, dtype=jnp.int32), pairs
    )
    summed = matmul_form("ca,csh->ash", cos_a, real) - matmul_form("ca,csh->ash", sin_a, imag)
    return summed * (1.0 / total)


def per_device(features, short_weights, doc_lengths, residues, rates, skip):
    seq_count = lax.axis_size("seq")
    chan_count = lax.axis_size("chan")
    seq_index = lax.axis_index("seq")
    chan_index = lax.axis_index("chan")
    tok_rows = features.shape[1]
    block = tok_rows * chan_count
    length = block * seq_count
    total = 2 * length
    pairs = 2 * seq_count
    rim = passed_along(features[:, tok_rows - (TAPS - 1) :, :], ("seq", "chan"), 1)
    first = (seq_index * chan_count + chan_index) * tok_rows
    streams = featurize(features, rim, short_weights, doc_lengths, first)
    gate = streams[0].astype(jnp.bfloat16)
    product = (streams[1] * streams[2]).astype(jnp.bfloat16)
    local = lax.all_to_all(
        jnp.stack([gate, product]), "chan", split_axis=2, concat_axis=1, tiled=True
    )
    width = local.shape[2]
    step = block // seq_count
    spread = lax.all_to_all(
        local[1].reshape(seq_count, step, width), "seq", split_axis=0, concat_axis=0, tiled=True
    )
    offsets = seq_index * step + jnp.arange(step, dtype=jnp.int32)
    real, imag = blocks_forward(spread.astype(jnp.float32), offsets, pairs, total)
    columns = lax.all_to_all(
        jnp.stack([real, imag]).astype(jnp.bfloat16), "seq", split_axis=1, concat_axis=2, tiled=True
    ).astype(jnp.float32)
    owned = 2 * seq_index + jnp.arange(2, dtype=jnp.int32)
    real, imag = spectral(columns[0], columns[1], owned, pairs, residues, rates, length)
    rows_back = lax.all_to_all(
        jnp.stack([real, imag]).astype(jnp.bfloat16), "seq", split_axis=2, concat_axis=1, tiled=True
    ).astype(jnp.float32)
    pieces = blocks_inverse(rows_back[0], rows_back[1], offsets, seq_count, total)
    conv = (
        lax.all_to_all(pieces.astype(jnp.bfloat16), "seq", split_axis=0, concat_axis=0, tiled=True)
        .astype(pieces.dtype)
        .reshape(block, width)
    )
    mixed = local[0].astype(jnp.float32) * (conv + skip[None, :] * local[1].astype(jnp.float32))
    return lax.all_to_all(
        mixed.astype(jnp.bfloat16), "chan", split_axis=0, concat_axis=1, tiled=True
    )


def solution(mesh):
    placed = (P(None, ("seq", "chan"), None), P(), P(), P(None, "chan"), P(None, "chan"), P("chan"))
    return jax.shard_map(
        per_device, mesh=mesh, in_specs=placed, out_specs=P(("seq", "chan"), None), check_vma=False
    )
```

profile of v0, /device:TPU:33, one launch (start us, length us, event | category | flops | bytes accessed | tf_op | source)
XLA Modules:
  0.0 514.7 jit_solution(11285569212024351888)
XLA Ops:
  1.3 3.1 collective-permute-start
  6.1 1.7 fusion.229
  8.1 26.5 %collective-permute-done = bf16[3,2,8192]{2,0,1:T(4,128)(2,1)S(1)} collective-permute-done((bf16[3,2,8192]{2,0,1:T(4,128)(2,1)S(1)}, bf16[3,2,8192]{2,0,1:T(4,128)(2,1)S(1)}, u32[]{:S(2)}, u32[]{:S(2)}) %collective-permute-start) | collective-permute-done | bytes 98336 | tf_op jit(solution)/shard_map/ppermute | solution.py:14
  36.9 6.7 %copy.243 = bf16[2,32,8192]{1,0,2:T(2,128)(2,1)} copy(bf16[2,32,8192]{2,1,0:T(8,128)(2,1)S(1)} %pad_maximum_fusion.2) | data formatting | bytes 2097152 | tf_op jit(solution)/shard_map/stack | solution.py:178
  43.6 9.3 %reshape.275 = bf16[32,2,8192]{2,1,0:T(2,128)(2,1)S(1)} reshape(bf16[8192,2,32]{2,1,0:T(2,128)(2,1)} %bitcast.159) | data formatting | bytes 2097152
  52.9 59.7 %all_to_all.65 = bf16[32,2,8192]{2,1,0:T(2,128)(2,1)S(1)} all-to-all(bf16[32,2,8192]{2,1,0:T(2,128)(2,1)S(1)} %reshape.275), channel_id=1, replica_groups=mesh['seq'=16,'chan'=32] {'chan'}, dimensions={0} | all-to-all | bytes 2097152 | tf_op jit(solution)/shard_map/all_to_all | solution.py:177
  112.6 3.5 reshape.276
  116.1 6.1 %copy.291 = bf16[2,32,32,256]{3,2,1,0:T(8,128)(2,1)S(1)} copy(bf16[2,32,32,256]{1,0,3,2:T(2,128)(2,1)} %bitcast.160) | data formatting | bytes 2097152 | tf_op jit(solution)/shard_map/all_to_all | solution.py:177
  123.3 3.7 all-to-all-start.1
  127.2 26.5 %all-to-all-done.1 = bf16[16,64,256]{2,1,0:T(8,128)(2,1)S(1)} async-done(((bf16[16,64,256]{2,1,0:T(8,128)(2,1)}), bf16[16,64,256]{2,1,0:T(8,128)(2,1)S(1)}, u32[]{:S(2)}, u32[]{:S(2)}) %all-to-all-start.1) | async-done | bytes 524320 | tf_op jit(solution)/shard_map/all_to_all | solution.py:182
  154.8 2.2 fusion.34
  157.2 2.5 copy.248
  159.8 7.1 %all-to-all-start.2 = ((bf16[2,32,64,256]{3,2,0,1:T(8,128)(2,1)}), bf16[2,32,64,256]{3,2,0,1:T(8,128)(2,1)S(1)}, u32[]{:S(2)}, u32[]{:S(2)}) async-start(bf16[2,32,64,256]{3,2,0,1:T(8,128)(2,1)} %copy.248), calls=%async_computation.2 | async-start | bytes 4194304 | tf_op jit(solution)/shard_map/all_to_all | solution.py:187
  167.4 21.0 %fusion.4 = (f32[2,8,128,256]{3,2,1,0:T(8,128)}, f32[2,8,128,256]{3,2,1,0:T(8,128)}) fusion(f32[2,8,128]{2,1,0:T(8,128)S(1)} %get-tuple-element.27, f32[2,8,128]{2,1,0:T(8,128)S(1)} %get-tuple-element.26, f32[16,256]{1,0:T(8,128)S(1)} %get-tuple-element.24, f32[16,256]{1,0:T(8,128)S(1)} %get-tuple-element.23, f32[16,256]{1,0:T(8,128)S(1)} %get-tuple-element.25, ...), kind=kLoop, calls=%fused_computation.6 | loop fusion | flops 124780544 | bytes 4284416 | tf_op jit(solution)/shard_map/reduce_sum | solution.py:61
  188.4 2.9 copy.267
  191.3 2.9 copy.264
  194.2 62.7 %all-to-all-done.2 = bf16[2,32,64,256]{3,2,0,1:T(8,128)(2,1)S(1)} async-done(((bf16[2,32,64,256]{3,2,0,1:T(8,128)(2,1)}), bf16[2,32,64,256]{3,2,0,1:T(8,128)(2,1)S(1)}, u32[]{:S(2)}, u32[]{:S(2)}) %all-to-all-start.2) | async-done | bytes 2097184 | tf_op jit(solution)/shard_map/all_to_all | solution.py:187
  257.5 1.4 fusion.44
  258.9 1.4 fusion.48
  260.3 1.5 convolution_add_fusion
  261.8 4.0 fusion.13
  265.8 2.0 copy.262
  267.8 3.4 copy.263
  271.2 3.6 fusion.65
  274.9 2.1 fusion.67
  277.1 2.1 convolution_add_fusion.2
  279.3 2.4 fusion.12
  281.7 2.1 fusion.61
  283.8 2.2 fusion.63
  286.0 2.2 convolution_add_fusion.1
  288.2 4.1 subtract_bitcast_fusion
  292.3 2.2 copy.269
  294.5 3.1 copy.270
  297.6 3.5 fusion.117
  301.1 1.9 fusion.119
  303.1 2.1 fusion.27
  305.1 2.1 fusion.26
  307.9 2.2 copy.275
  310.1 103.1 %all_to_all.66 = bf16[2,2,1024,256]{3,1,0,2:T(2,128)(2,1)S(1)} all-to-all(bf16[2,2,1024,256]{3,1,0,2:T(2,128)(2,1)S(1)} %copy.275), channel_id=1, replica_groups=mesh['seq'=16,'chan'=32] {'seq'}, dimensions={2} | all-to-all | bytes 4194304 | tf_op jit(solution)/shard_map/all_to_all | solution.py:192
  414.0 1.7 fusion.227
  415.7 2.9 copy.278
  418.6 2.7 squeeze.5
  421.3 4.5 copy.277
  425.8 3.7 squeeze.4
  429.5 3.1 fusion.15
  432.6 1.8 fusion.31
  434.6 33.0 %all_to_all.67 = bf16[16,64,256]{2,1,0:T(8,128)(2,1)S(1)} all-to-all(bf16[16,64,256]{2,1,0:T(8,128)(2,1)S(1)} %copy.279), channel_id=1, replica_groups=mesh['seq'=16,'chan'=32] {'seq'}, dimensions={0} | all-to-all | bytes 1048576 | tf_op jit(solution)/shard_map/all_to_all | solution.py:197
  468.7 44.8 %all_to_all.68 = bf16[32,32,256]{2,1,0:T(8,128)(2,1)S(1)} all-to-all(bf16[32,32,256]{2,1,0:T(8,128)(2,1)S(1)} %copy.281), channel_id=1, replica_groups=mesh['seq'=16,'chan'=32] {'chan'}, dimensions={0} | all-to-all | bytes 1048576 | tf_op jit(solution)/shard_map/all_to_all | solution.py:202
  (64 shorter events, 12.7 us)
Async XLA Ops:
  0.0 34.7 %copy-start.5 = (bf16[3,32,8192]{2,1,0:T(8,128)(2,1)S(1)}, bf16[3,32,8192]{2,1,0:T(8,128)(2,1)}, u32[]{:S(2)}) copy-start(bf16[3,32,8192]{2,1,0:T(8,128)(2,1)} %param.6) | copy-start | bytes 4718596
  1.3 33.3 %collective-permute-start = (bf16[3,2,8192]{2,0,1:T(4,128)(2,1)S(1)}, bf16[3,2,8192]{2,0,1:T(4,128)(2,1)S(1)}, u32[]{:S(2)}, u32[]{:S(2)}) collective-permute-start(bf16[3,2,8192]{2,0,1:T(4,128)(2,1)S(1)} %copy.299), channel_id=1, source_target_pairs={{0,1},{1,2},{2,3},{3,4},{4,5},{5,6},{6,7},{7,8},{8,9},{9,10},{10,1... | collective-permute-start | bytes 294920 | tf_op jit(solution)/shard_map/ppermute | solution.py:14
  123.3 30.4 %all-to-all-start.1 = ((bf16[16,64,256]{2,1,0:T(8,128)(2,1)}), bf16[16,64,256]{2,1,0:T(8,128)(2,1)S(1)}, u32[]{:S(2)}, u32[]{:S(2)}) async-start(bf16[16,64,256]{2,1,0:T(8,128)(2,1)} %bitcast.5), calls=%async_computation.1 | async-start | bytes 1048576 | tf_op jit(solution)/shard_map/all_to_all | solution.py:182
  159.8 7.6 %copy-start.6 = (f32[16,256]{1,0:T(8,128)S(1)}, f32[16,256]{1,0:T(8,128)}, u32[]{:S(2)}) copy-start(f32[16,256]{1,0:T(8,128)} %param.9) | copy-start | bytes 49156
  159.8 7.6 %copy-start.7 = (f32[16,256]{1,0:T(8,128)S(1)}, f32[16,256]{1,0:T(8,128)}, u32[]{:S(2)}) copy-start(f32[16,256]{1,0:T(8,128)} %param.10) | copy-start | bytes 49156
  159.8 97.2 %all-to-all-start.2 = ((bf16[2,32,64,256]{3,2,0,1:T(8,128)(2,1)}), bf16[2,32,64,256]{3,2,0,1:T(8,128)(2,1)S(1)}, u32[]{:S(2)}, u32[]{:S(2)}) async-start(bf16[2,32,64,256]{3,2,0,1:T(8,128)(2,1)} %copy.248), calls=%async_computation.2 | async-start | bytes 4194304 | tf_op jit(solution)/shard_map/all_to_all | solution.py:187
  274.9 2.2 copy-start
  277.0 2.1 copy-start.3
  277.1 2.2 copy-start.4
  303.0 2.1 copy-start.1
  429.5 3.1 copy-start.2
  434.4 33.3 %copy-start.8 = (f32[256]{0:T(256)S(1)}, f32[256]{0:T(256)}, u32[]{:S(2)}) copy-start(f32[256]{0:T(256)} %param.11) | copy-start | bytes 3076
where the time goes:
time: 524 us; the launch traced here: 515 us
  blocking collectives  241 us (46%)
  waiting for transfers between devices  116 us (22%)
  local copies, waits for them, and re-layouts  70.4 us (13%)
  matrix products  46.9 us (9%)
  other arithmetic  26.3 us (5%)
  starting transfers between devices  13.9 us (3%)
    all_to_all x1, blocking collectives, per_device(): lax.all_to_all(jnp.stack([real, imag]).astype(jnp.bfloat16), 'seq', split...  103 us
    all_to_all x1, waiting for transfers between devices, per_device(): lax.all_to_all(jnp.stack([real, imag]).astype(jnp.bfloat16), 'seq', split...  62.7 us
    all_to_all x1, blocking collectives, per_device(): lax.all_to_all(jnp.stack([gate, product]), 'chan', split_axis=2, concat_a...  59.7 us
    dot_general x20, matrix products, matmul_form(): jnp.einsum(form, table, data, precision=lax.Precision.HIGHEST, preferred_...  46.9 us
    all_to_all x1, blocking collectives, per_device(): lax.all_to_all(mixed.astype(jnp.bfloat16), 'chan', split_axis=0, concat_a...  44.8 us
    all_to_all x1, blocking collectives, per_device(): lax.all_to_all(pieces.astype(jnp.bfloat16), 'seq', split_axis=0, concat_a...  33 us
    ppermute x1, waiting for transfers between devices, passed_along(): return lax.ppermute(x, axis, pairs)  26.5 us
    all_to_all x1, waiting for transfers between devices, per_device(): lax.all_to_all(local[1].reshape(seq_count, step, width), 'seq', split_axi...  26.5 us
  transfers between devices with their start and end apart: 3, of which 3 were waited for; matrix products, arithmetic and copies ran while one was open for 6% of the time, Pallas kernels for 0%

commit v1 on v0

v1 whole, which is shorter than its diff:
```python
import functools

import jax
import jax.numpy as jnp
from jax import lax
from jax.experimental import pallas as pl
from jax.experimental.pallas import tpu as pltpu
from jax.sharding import PartitionSpec as P

MODES = 16
LANES = 128
QUADS = 4
HALF = 256
VMEM = pl.BlockSpec(memory_space=pltpu.VMEM)
PARAMS = pltpu.CompilerParams(vmem_limit_bytes=48 * 2**20)


def doc_starts(doc_ref):
    n = doc_ref.shape[1]
    lengths = doc_ref[...].astype(jnp.float32)
    rows = lax.broadcasted_iota(jnp.int32, (n, n), 0)
    cols = lax.broadcasted_iota(jnp.int32, (n, n), 1)
    wide = jnp.broadcast_to(lengths, (n, n))
    column = jnp.sum(jnp.where(rows == cols, wide, 0.0), axis=1, keepdims=True)
    return jnp.sum(jnp.where(rows < cols, column, 0.0), axis=0, keepdims=True)


def featurize(first, doc_ref, feat_ref, rim_ref, short_ref, gate_ref, prod_ref):
    rows = feat_ref.shape[1]
    peers = prod_ref.shape[0]
    starts = doc_starts(doc_ref)
    n = starts.shape[1]
    index = lax.broadcasted_iota(jnp.int32, (rows, n), 0)
    position = (first + index).astype(jnp.float32)
    here = jnp.max(jnp.where(starts == position, 1.0, 0.0), axis=1, keepdims=True)
    before = jnp.max(jnp.where(starts == position - 1.0, 1.0, 0.0), axis=1, keepdims=True)
    one = jnp.broadcast_to(here, (rows, HALF)) < 0.5
    two = jnp.broadcast_to(here + before, (rows, HALF)) < 0.5
    row = lax.broadcasted_iota(jnp.int32, (rows, HALF), 0)

    @pl.loop(0, 2 * peers)
    def _(block):
        cols = pl.ds(pl.multiple_of(block * HALF, HALF), HALF)
        streams = []
        for s in range(3):
            x = feat_ref[s, :, cols].astype(jnp.float32)
            rim = rim_ref[s, :, cols].astype(jnp.float32)
            x1 = jnp.where(row == 0, rim[1:2], pltpu.roll(x, 1, 0))
            x2 = jnp.where(row == 0, rim[0:1], jnp.where(row == 1, rim[1:2], pltpu.roll(x, 2, 0)))
            streams.append(
                x * short_ref[s, 0:1, cols]
                + jnp.where(one, x1, 0.0) * short_ref[s, 1:2, cols]
                + jnp.where(two, x2, 0.0) * short_ref[s, 2:3, cols]
            )
        gate_ref[:, cols] = streams[0].astype(jnp.bfloat16)
        value = (streams[1] * streams[2]).astype(jnp.bfloat16)

        @pl.when(block < peers)
        def _():
            prod_ref[block, :, 0:HALF] = value

        @pl.when(block >= peers)
        def _():
            prod_ref[block - peers, :, HALF : 2 * HALF] = value


def scatter_params(modes_ref, rate_ref, gain_ref, skip_ref):
    for q in range(QUADS):
        cols = slice((q % 2) * LANES, (q % 2 + 1) * LANES)
        rate = modes_ref[q // 2, 0:MODES, cols]
        gain = modes_ref[q // 2, MODES : 2 * MODES, cols]
        skip = modes_ref[q // 2, 2 * MODES : 2 * MODES + 1, cols]
        for h in range(2):
            at = h * QUADS + q
            rate_ref[pl.ds(at, MODES, stride=8), :] = rate
            gain_ref[pl.ds(at, MODES, stride=8), :] = gain
            skip_ref[at : at + 1, :] = skip


def spread(recv_ref, u_ref):
    peers, rows, _ = recv_ref.shape
    steps = peers * rows // 2

    @pl.loop(0, peers)
    def _(p):
        h = p // (peers // 2)
        t = (p % (peers // 2)) * rows
        for q in range(QUADS):
            at = pl.multiple_of((h * QUADS + q) * steps + t, 32)
            u_ref[pl.ds(at, rows), :] = recv_ref[p, :, q * LANES : (q + 1) * LANES].astype(jnp.float32)


def mode_rows(ref):
    return [ref[m * 8 : m * 8 + 8, :] for m in range(MODES)]


def local_states(u_ref, rate_ref, end_ref, steps):
    decay = [jnp.exp(-x) for x in mode_rows(rate_ref)]

    def step(t, x):
        u = u_ref[pl.ds(t, 8, stride=steps), :]
        return tuple(d * a + u for d, a in zip(decay, x))

    zero = jnp.zeros((8, LANES), jnp.float32)
    x = lax.fori_loop(0, steps, step, (zero,) * MODES, unroll=8)
    for m in range(MODES):
        end_ref[m * 8 : m * 8 + 8, :] = x[m]


def block_states(end_ref, rate_ref, state_ref, steps):
    for m in range(MODES):
        x = end_ref[m * 8 : m * 8 + 8, :]
        rate = rate_ref[m * 8 : m * 8 + 4, :]
        state_ref[m * 4 : m * 4 + 4, :] = jnp.exp(-float(steps) * rate) * x[0:4] + x[4:8]


def local_outputs(u_ref, rate_ref, gain_ref, skip_ref, y_ref, steps):
    decay = [jnp.exp(-x) for x in mode_rows(rate_ref)]
    gain = mode_rows(gain_ref)
    skip = skip_ref[...]

    def step(t, x):
        u = u_ref[pl.ds(t, 8, stride=steps), :]
        x = tuple(d * a + u for d, a in zip(decay, x))
        parts = [g * a for g, a in zip(gain, x)] + [skip * u]
        while len(parts) > 1:
            parts = [sum(parts[i : i + 2]) for i in range(0, len(parts), 2)]
        y_ref[pl.ds(t, 8, stride=steps), :] = parts[0]
        return x

    zero = jnp.zeros((8, LANES), jnp.float32)
    lax.fori_loop(0, steps, step, (zero,) * MODES, unroll=4)


def carried(end_ref, carry_ref, rate_ref, gain_ref, steps):
    out = []
    for m in range(MODES):
        carry = carry_ref[m * 4 : m * 4 + 4, :]
        rate = rate_ref[m * 8 : m * 8 + 4, :]
        later = end_ref[m * 8 : m * 8 + 4, :] + jnp.exp(-float(steps) * rate) * carry
        out.append(gain_ref[m * 8 : m * 8 + 8, :] * jnp.concatenate([carry, later], axis=0))
    return tuple(out)


def add_carried(state, decay, y_ref, t, steps):
    state = tuple(d * a for d, a in zip(decay, state))
    parts = list(state)
    while len(parts) > 1:
        parts = [sum(parts[i : i + 2]) for i in range(0, len(parts), 2)]
    rows = pl.ds(t, 8, stride=steps)
    y_ref[rows, :] = y_ref[rows, :] + parts[0]
    return state


def gathered(y_ref, out_ref, p, h, t, rows, steps):
    for q in range(QUADS):
        at = pl.multiple_of((h * QUADS + q) * steps + t, 32)
        out_ref[p, :, q * LANES : (q + 1) * LANES] = y_ref[pl.ds(at, rows), :].astype(jnp.bfloat16)


def featurize_kernel(doc_ref, feat_ref, rim_ref, short_ref, gate_ref, prod_ref):
    me = lax.axis_index("seq") * lax.axis_size("chan") + lax.axis_index("chan")
    featurize(me * feat_ref.shape[1], doc_ref, feat_ref, rim_ref, short_ref, gate_ref, prod_ref)


def filter_kernel(recv_ref, modes_ref, state_ref, end_ref, y_ref, u_ref, rate_ref, gain_ref, skip_ref):
    steps = recv_ref.shape[0] * recv_ref.shape[1] // 2
    scatter_params(modes_ref, rate_ref, gain_ref, skip_ref)
    spread(recv_ref, u_ref)
    local_states(u_ref, rate_ref, end_ref, steps)
    block_states(end_ref, rate_ref, state_ref, steps)
    local_outputs(u_ref, rate_ref, gain_ref, skip_ref, y_ref, steps)


def finish_kernel(all_ref, end_ref, yin_ref, modes_ref, out_ref, y_ref, rate_ref, gain_ref, skip_ref, carry_ref):
    peers, rows, _ = out_ref.shape
    steps = peers * rows // 2
    scatter_params(modes_ref, rate_ref, gain_ref, skip_ref)
    me = lax.axis_index("seq") * 2 + lax.axis_index("chan") // peers
    decay = [jnp.exp(-2.0 * steps * rate_ref[m * 8 : m * 8 + 4, :]) for m in range(MODES)]

    def earlier(b, x):
        s = all_ref[b]
        return tuple(
            jnp.where(b < me, d * a + s[m * 4 : m * 4 + 4, :], a)
            for m, (d, a) in enumerate(zip(decay, x))
        )

    zero = jnp.zeros((QUADS, LANES), jnp.float32)
    x = lax.fori_loop(0, all_ref.shape[0], earlier, (zero,) * MODES)
    for m in range(MODES):
        carry_ref[m * 4 : m * 4 + 4, :] = x[m]
    y_ref[...] = yin_ref[...]
    state = carried(end_ref, carry_ref, rate_ref, gain_ref, steps)
    decay = [jnp.exp(-x) for x in mode_rows(rate_ref)]

    def part(i, state):
        state = lax.fori_loop(
            0, rows, lambda t, s: add_carried(s, decay, y_ref, i * rows + t, steps), state, unroll=8
        )
        for h in range(2):
            gathered(y_ref, out_ref, h * (peers // 2) + i, h, i * rows, rows, steps)
        return state

    lax.fori_loop(0, peers // 2, part, state)


def per_device(features, short_weights, doc_lengths, residues, rates, skip):
    seqs = lax.axis_size("seq")
    chans = lax.axis_size("chan")
    peers = chans // 2
    blocks = 2 * seqs
    rows, width = features.shape[1:]
    steps = peers * rows // 2
    bf16, f32 = jnp.bfloat16, jnp.float32
    sds = jax.ShapeDtypeStruct
    chan = lax.axis_index("chan")

    count = seqs * chans
    rim = lax.ppermute(
        features[:, rows - 2 :, :], ("seq", "chan"), [(i, (i + 1) % count) for i in range(count)]
    )
    gains = residues * jnp.sqrt(-jnp.expm1(-2.0 * rates))
    mine = jnp.concatenate([rates, gains, jnp.pad(skip[None, :], ((0, 7), (0, 0)))])
    other = lax.ppermute(mine, "chan", [(i, (i + peers) % chans) for i in range(chans)])
    modes = jnp.where(chan < peers, jnp.stack([mine, other]), jnp.stack([other, mine]))

    gate, product = pl.pallas_call(
        featurize_kernel,
        out_shape=(sds((rows, width), bf16), sds((peers, rows, 2 * HALF), bf16)),
        in_specs=[VMEM] * 4,
        out_specs=(VMEM, VMEM),
        compiler_params=PARAMS,
    )(doc_lengths[None, :], features, rim, short_weights)
    plane = [[z * peers + p for p in range(peers)] for z in range(2)]
    received = lax.all_to_all(product, "chan", 0, 0, axis_index_groups=plane, tiled=True)
    wide = (2 * QUADS * steps, LANES)
    table = pltpu.VMEM((8 * MODES, LANES), f32)
    state, end, local = pl.pallas_call(
        filter_kernel,
        out_shape=(sds((MODES * QUADS, LANES), f32), sds((8 * MODES, LANES), f32), sds(wide, f32)),
        in_specs=[VMEM] * 2,
        out_specs=(VMEM,) * 3,
        scratch_shapes=[pltpu.VMEM(wide, f32), table, table, pltpu.VMEM((8, LANES), f32)],
        compiler_params=PARAMS,
    )(received, modes)
    column = [
        [s * chans + z * peers + p for s in range(seqs) for z in range(2)] for p in range(peers)
    ]
    states = lax.all_gather(state, ("seq", "chan"), axis_index_groups=column)
    mixed = pl.pallas_call(
        finish_kernel,
        out_shape=sds((peers, rows, 2 * HALF), bf16),
        in_specs=[VMEM] * 4,
        out_specs=VMEM,
        scratch_shapes=[
            pltpu.VMEM(wide, f32),
            table,
            table,
            pltpu.VMEM((8, LANES), f32),
            pltpu.VMEM((MODES * QUADS, LANES), f32),
        ],
        compiler_params=PARAMS,
    )(states, end, local, modes)
    back = lax.all_to_all(mixed, "chan", 0, 0, axis_index_groups=plane, tiled=True)
    back = back.reshape(peers, rows, 2, HALF).transpose(1, 2, 0, 3).reshape(rows, width)
    return (gate.astype(f32) * back.astype(f32)).astype(bf16)


def solution(mesh):
    placed = (P(None, ("seq", "chan"), None), P(), P(), P(None, "chan"), P(None, "chan"), P("chan"))
    return jax.shard_map(
        per_device, mesh=mesh, in_specs=placed, out_specs=P(("seq", "chan"), None), check_vma=False
    )
```

time: 524 us -> 344 us (0.66)
  the two profiles are of different devices: /device:TPU:33 before, /device:TPU:1 now
where the time goes in v1:
time: 344 us; the launch traced here: 343 us
  waiting for transfers between devices  276 us (80%)
  starting transfers between devices  21.4 us (6%)
  between operations  13.5 us (4%)
  blocking collectives  13.1 us (4%)
  Pallas kernels  11.1 us (3%)
  local copies, waits for them, and re-layouts  7.27 us (2%)
    all_gather x1, waiting for transfers between devices, per_device(): states = lax.all_gather(state, ('seq', 'chan'), axis_index_groups=column)  254 us
    ppermute x1, waiting for transfers between devices, per_device(): lax.ppermute(features[:, rows - 2:, :], ('seq', 'chan'), [(i, (i + 1) % c...  19.9 us
    ppermute x1, starting transfers between devices, per_device(): lax.ppermute(mine, 'chan', [(i, (i + peers) % chans) for i in range(chans)])  13.9 us
    all_to_all x1, blocking collectives, per_device(): lax.all_to_all(mixed, 'chan', 0, 0, axis_index_groups=plane, tiled=True)  13.1 us
  transfers between devices with their start and end apart: 4, of which 3 were waited for; matrix products, arithmetic and copies ran while one was open for 0% of the time, Pallas kernels for 0%

profile of v1, /device:TPU:1, one launch (start us, length us, event | category | flops | bytes accessed | tf_op | source)
XLA Modules:
  0.0 343.1 jit_solution(15938401683432860024)
XLA Ops:
  6.5 0.0 copy-start.4
  6.5 0.0 copy-start.5
  6.5 1.1 slice.3
  7.7 3.9 %collective-permute-start = (bf16[3,2,8192]{2,1,0:T(2,128)(2,1)S(1)}, bf16[3,2,8192]{2,1,0:T(2,128)(2,1)S(1)}, u32[]{:S(2)}, u32[]{:S(2)}) collective-permute-start(bf16[3,2,8192]{2,1,0:T(2,128)(2,1)S(1)} %slice.3), channel_id=1, source_target_pairs={{0,1},{1,2},{2,3},{3,4},{4,5},{5,6},{6,7},{7,8},{8,9},{9,10},{10,1... | collective-permute-start | bytes 294920 | tf_op jit(solution)/shard_map/ppermute | solution.py:220
  11.6 19.9 %collective-permute-done.rim_ref = bf16[3,2,8192]{2,1,0:T(2,128)(2,1)S(1)} collective-permute-done((bf16[3,2,8192]{2,1,0:T(2,128)(2,1)S(1)}, bf16[3,2,8192]{2,1,0:T(2,128)(2,1)S(1)}, u32[]{:S(2)}, u32[]{:S(2)}) %collective-permute-start) | collective-permute-done | bytes 98336 | tf_op jit(solution)/shard_map/ppermute | solution.py:220
  31.5 0.0 copy-start
  31.5 1.4 copy-done
  32.9 0.0 copy-start.2
  32.9 1.0 copy-done.2
  33.9 0.0 copy-start.3
  33.9 0.7 copy-done.3
  34.6 0.0 copy-start.6
  34.6 3.0 shard_map.64
  37.6 3.6 %all-to-all-start = ((bf16[16,32,512]{2,1,0:T(8,128)(2,1)}), bf16[16,32,512]{2,1,0:T(8,128)(2,1)S(1)}, u32[]{:S(2)}, u32[]{:S(2)}) async-start(bf16[16,32,512]{2,1,0:T(8,128)(2,1)} %get-tuple-element.11), calls=%async_computation | async-start | bytes 1048576 | tf_op jit(solution)/shard_map/all_to_all | solution.py:236
  41.2 0.0 all-gather.3.cloned.1.call-start
  41.2 0.0 copy-done.4
  41.3 0.0 copy-done.5
  41.3 0.0 copy-done.6
  41.3 13.9 %collective-permute-start.1 = (f32[40,256]{1,0:T(8,128)S(1)}, f32[40,256]{1,0:T(8,128)S(1)}, u32[]{:S(2)}, u32[]{:S(2)}) collective-permute-start(f32[40,256]{1,0:T(8,128)S(1)} %get-tuple-element.16), channel_id=1, source_target_pairs={{0,16},{1,17},{2,18},{3,19},{4,20},{5,21},{6,22},{7,23},{8,24},{9,... | collective-permute-start | bytes 122888 | tf_op jit(solution)/shard_map/ppermute | solution.py:225
  55.2 1.4 collective-permute-done.1
  56.6 0.0 all-to-all-done.recv_ref
  56.6 5.8 %shard_map.65 = (f32[64,128]{1,0:T(8,128)}, f32[128,128]{1,0:T(8,128)S(1)}, f32[2048,128]{1,0:T(8,128)S(1)}) custom-call(bf16[16,32,512]{2,1,0:T(8,128)(2,1)S(1)} %all-to-all-done.recv_ref, f32[2,40,256]{2,1,0:T(8,128)S(1)} %maximum_select_fusion.modes_ref), custom_call_target="tpu_custom_call" | custom-call | tf_op jit(solution)/shard_map/pallas_call | solution.py:239
  62.4 0.0 all-gather.3.cloned.1.call-update
  62.4 254.4 %all-gather.3.cloned.1.call-done = f32[2048,128]{1,0:T(8,128)} async-done(((f32[64,128]{1,0:T(8,128)}), f32[2048,128]{1,0:T(8,128)}) %all-gather.3.cloned.1.call-update) | async-done | bytes 1048592 | tf_op jit(solution)/shard_map/all_gather | solution.py:250
  316.8 0.0 copy-start.1
  316.8 1.2 copy-done.1
  318.1 2.3 shard_map.66
  320.3 13.1 %all_to_all.10 = bf16[16,32,512]{2,1,0:T(8,128)(2,1)S(1)} all-to-all(bf16[16,32,512]{2,1,0:T(8,128)(2,1)S(1)} %shard_map.66), channel_id=1, replica_groups={{0,1,2,3,4,5,6,7,8,9,10,11,12,13,14,15},{16,17,18,19,20,21,22,23,24,25,..., dimensions={0} | all-to-all | bytes 1048576 | tf_op jit(solution)/shard_map/all_to_all | solution.py:265
  333.5 0.6 reshape.7
  334.1 0.6 copy.7
  334.7 0.6 copy.8
  335.4 0.9 multiply_convert_fusion
  (3 shorter events, 0.0 us)
Async XLA Ops:
  6.5 34.7 %copy-start.4 = (f32[16,256]{1,0:T(8,128)S(1)}, f32[16,256]{1,0:T(8,128)}, u32[]{:S(2)}) copy-start(f32[16,256]{1,0:T(8,128)} %param.10) | copy-start | bytes 49156
  6.5 34.7 %copy-start.5 = (f32[16,256]{1,0:T(8,128)S(1)}, f32[16,256]{1,0:T(8,128)}, u32[]{:S(2)}) copy-start(f32[16,256]{1,0:T(8,128)} %param.9) | copy-start | bytes 49156
  7.7 23.9 %collective-permute-start = (bf16[3,2,8192]{2,1,0:T(2,128)(2,1)S(1)}, bf16[3,2,8192]{2,1,0:T(2,128)(2,1)S(1)}, u32[]{:S(2)}, u32[]{:S(2)}) collective-permute-start(bf16[3,2,8192]{2,1,0:T(2,128)(2,1)S(1)} %slice.3), channel_id=1, source_target_pairs={{0,1},{1,2},{2,3},{3,4},{4,5},{5,6},{6,7},{7,8},{8,9},{9,10},{10,1... | collective-permute-start | bytes 294920 | tf_op jit(solution)/shard_map/ppermute | solution.py:220
  31.5 1.4 copy-start
  32.9 1.0 copy-start.2
  33.9 0.7 copy-start.3
  34.6 6.7 %copy-start.6 = (f32[256]{0:T(256)S(1)}, f32[256]{0:T(256)}, u32[]{:S(2)}) copy-start(f32[256]{0:T(256)} %param.11) | copy-start | bytes 3076
  37.6 19.0 %all-to-all-start = ((bf16[16,32,512]{2,1,0:T(8,128)(2,1)}), bf16[16,32,512]{2,1,0:T(8,128)(2,1)S(1)}, u32[]{:S(2)}, u32[]{:S(2)}) async-start(bf16[16,32,512]{2,1,0:T(8,128)(2,1)} %get-tuple-element.11), calls=%async_computation | async-start | bytes 1048576 | tf_op jit(solution)/shard_map/all_to_all | solution.py:236
  41.2 275.6 %all-gather.3.cloned.1.call-start = ((), (), s32[]{:S(2)}) async-start(), calls=%async_computation.2 | async-start | bytes 1081344 | tf_op jit(solution)/shard_map/all_gather | solution.py:250
  41.3 15.2 %collective-permute-start.1 = (f32[40,256]{1,0:T(8,128)S(1)}, f32[40,256]{1,0:T(8,128)S(1)}, u32[]{:S(2)}, u32[]{:S(2)}) collective-permute-start(f32[40,256]{1,0:T(8,128)S(1)} %get-tuple-element.16), channel_id=1, source_target_pairs={{0,16},{1,17},{2,18},{3,19},{4,20},{5,21},{6,22},{7,23},{8,24},{9,... | collective-permute-start | bytes 122888 | tf_op jit(solution)/shard_map/ppermute | solution.py:225
  316.8 1.2 copy-start.1
Sparse Core Ops, SparseCore 0:
  62.6 254.2 all-gather.2

commit v2 on v1

v2 whole, which is shorter than its diff:
```python
import jax
import jax.numpy as jnp
from jax import lax
from jax.experimental import pallas as pl
from jax.experimental.pallas import tpu as pltpu
from jax.sharding import PartitionSpec as P

MODES = 16
LANES = 128
QUADS = 4
HALF = 256
VMEM = pl.BlockSpec(memory_space=pltpu.VMEM)
MESH = pl.DeviceIdType.MESH


def doc_starts(doc_ref):
    n = doc_ref.shape[1]
    lengths = doc_ref[...].astype(jnp.float32)
    rows = lax.broadcasted_iota(jnp.int32, (n, n), 0)
    cols = lax.broadcasted_iota(jnp.int32, (n, n), 1)
    wide = jnp.broadcast_to(lengths, (n, n))
    column = jnp.sum(jnp.where(rows == cols, wide, 0.0), axis=1, keepdims=True)
    return jnp.sum(jnp.where(rows < cols, column, 0.0), axis=0, keepdims=True)


def tap_masks(first, doc_ref, rows):
    starts = doc_starts(doc_ref)
    n = starts.shape[1]
    index = lax.broadcasted_iota(jnp.int32, (rows, n), 0)
    position = (first + index).astype(jnp.float32)
    here = jnp.max(jnp.where(starts == position, 1.0, 0.0), axis=1, keepdims=True)
    before = jnp.max(jnp.where(starts == position - 1.0, 1.0, 0.0), axis=1, keepdims=True)
    one = jnp.broadcast_to(here, (rows, HALF)) < 0.5
    two = jnp.broadcast_to(here + before, (rows, HALF)) < 0.5
    return one, two


def featurize(block, one, two, feat_ref, rim_ref, short_ref, gate_ref):
    row = lax.broadcasted_iota(jnp.int32, one.shape, 0)
    cols = pl.ds(pl.multiple_of(block * HALF, HALF), HALF)
    streams = []
    for s in range(3):
        x = feat_ref[s, :, cols].astype(jnp.float32)
        rim = rim_ref[s, :, cols].astype(jnp.float32)
        x1 = jnp.where(row == 0, rim[1:2], pltpu.roll(x, 1, 0))
        x2 = jnp.where(row == 0, rim[0:1], jnp.where(row == 1, rim[1:2], pltpu.roll(x, 2, 0)))
        streams.append(
            x * short_ref[s, 0:1, cols]
            + jnp.where(one, x1, 0.0) * short_ref[s, 1:2, cols]
            + jnp.where(two, x2, 0.0) * short_ref[s, 2:3, cols]
        )
    gate_ref[:, cols] = streams[0].astype(jnp.bfloat16)
    return (streams[1] * streams[2]).astype(jnp.bfloat16)


def mode_gain(rate, residue):
    x = 2.0 * rate
    series = jnp.ones_like(x)
    for n in range(9, 1, -1):
        series = 1.0 - x * (1.0 / n) * series
    return residue * jnp.sqrt(x * series)


def scatter_params(modes_ref, rate_ref, gain_ref, skip_ref):
    for q in range(QUADS):
        cols = slice((q % 2) * LANES, (q % 2 + 1) * LANES)
        rate = modes_ref[q // 2, 0:MODES, cols]
        gain = modes_ref[q // 2, MODES : 2 * MODES, cols]
        skip = modes_ref[q // 2, 2 * MODES : 2 * MODES + 1, cols]
        for h in range(2):
            at = h * QUADS + q
            rate_ref[pl.ds(at, MODES, stride=8), :] = rate
            gain_ref[pl.ds(at, MODES, stride=8), :] = gain
            skip_ref[at : at + 1, :] = skip


def spread(p, recv_ref, u_ref):
    peers, rows, _ = recv_ref.shape
    steps = peers * rows // 2
    h = p // (peers // 2)
    t = (p % (peers // 2)) * rows
    for q in range(QUADS):
        at = pl.multiple_of((h * QUADS + q) * steps + t, 32)
        u_ref[pl.ds(at, rows), :] = recv_ref[p, :, q * LANES : (q + 1) * LANES].astype(jnp.float32)


def mode_rows(ref):
    return [ref[m * 8 : m * 8 + 8, :] for m in range(MODES)]


def local_states(u_ref, rate_ref, end_ref, steps):
    decay = [jnp.exp(-x) for x in mode_rows(rate_ref)]

    def step(t, x):
        u = u_ref[pl.ds(t, 8, stride=steps), :]
        return tuple(d * a + u for d, a in zip(decay, x))

    zero = jnp.zeros((8, LANES), jnp.float32)
    x = lax.fori_loop(0, steps, step, (zero,) * MODES, unroll=8)
    for m in range(MODES):
        end_ref[m * 8 : m * 8 + 8, :] = x[m]


def block_states(end_ref, rate_ref, state_ref, steps):
    height = state_ref.shape[1]
    for m in range(MODES):
        x = end_ref[m * 8 : m * 8 + 8, :]
        rate = rate_ref[m * 8 : m * 8 + 4, :]
        state = jnp.exp(-float(steps) * rate) * x[0:4] + x[4:8]
        put_rows(state_ref, m, state)


def put_rows(ref, m, value):
    height = ref.shape[1]
    if height <= QUADS:
        for i in range(QUADS // height):
            ref[m * (QUADS // height) + i] = value[i * height : (i + 1) * height]
    else:
        each = height // QUADS
        ref[m // each, (m % each) * QUADS : (m % each + 1) * QUADS, :] = value


def get_rows(ref, m):
    height = ref.shape[1]
    if height <= QUADS:
        n = QUADS // height
        return jnp.concatenate([ref[m * n + i] for i in range(n)], axis=0)
    each = height // QUADS
    return ref[m // each, (m % each) * QUADS : (m % each + 1) * QUADS, :]


def local_outputs(x, begin, end, u_ref, rate_ref, gain_ref, skip_ref, y_ref, steps):
    decay = [jnp.exp(-x) for x in mode_rows(rate_ref)]
    gain = mode_rows(gain_ref)
    skip = skip_ref[...]

    def step(t, x):
        u = u_ref[pl.ds(t, 8, stride=steps), :]
        x = tuple(d * a + u for d, a in zip(decay, x))
        y_ref[pl.ds(t, 8, stride=steps), :] = total([g * a for g, a in zip(gain, x)] + [skip * u])
        return x

    return lax.fori_loop(begin, end, step, x, unroll=4)


def total(parts):
    while len(parts) > 1:
        parts = [sum(parts[i : i + 2]) for i in range(0, len(parts), 2)]
    return parts[0]


def carried(end_ref, carry_ref, rate_ref, gain_ref, base_ref, steps):
    for m in range(MODES):
        carry = get_rows(carry_ref, m)
        rate = rate_ref[m * 8 : m * 8 + 4, :]
        later = end_ref[m * 8 : m * 8 + 4, :] + jnp.exp(-float(steps) * rate) * carry
        both = jnp.concatenate([carry, later], axis=0)
        base_ref[m * 8 : m * 8 + 8, :] = gain_ref[m * 8 : m * 8 + 8, :] * both


def add_carried(i, rows, base_ref, rate_ref, y_ref, steps):
    rate = mode_rows(rate_ref)
    decay = [jnp.exp(-x) for x in rate]
    begin = i * rows
    past = begin.astype(jnp.float32)
    state = tuple(a * jnp.exp(-past * r) for a, r in zip(mode_rows(base_ref), rate))

    def step(t, state):
        state = tuple(d * a for d, a in zip(decay, state))
        at = pl.ds(begin + t, 8, stride=steps)
        y_ref[at, :] = y_ref[at, :] + total(list(state))
        return state

    lax.fori_loop(0, rows, step, state, unroll=8)


def gathered(y_ref, out_ref, p, h, t, rows, steps):
    for q in range(QUADS):
        at = pl.multiple_of((h * QUADS + q) * steps + t, 32)
        out_ref[p, :, q * LANES : (q + 1) * LANES] = y_ref[pl.ds(at, rows), :].astype(jnp.bfloat16)


def kernel(
    doc_ref, feat_ref, short_ref, residues_ref, rates_ref, skipin_ref,
    out_ref,
    rim_ref, rimin_ref, modes_ref, gate_ref, prod_ref, recv_ref, u_ref, y_ref, mixed_ref, back_ref,
    rate_ref, gain_ref, skip_ref, end_ref, base_ref, state_ref, states_ref, carries_ref, carry_ref, fade_ref,
    pair_send, pair_recv, there_send, there_recv, back_send, back_recv, ring_send, ring_recv,
):
    seqs, chans = lax.axis_size("seq"), lax.axis_size("chan")
    seq, chan = lax.axis_index("seq"), lax.axis_index("chan")
    peers, rows, _ = prod_ref.shape
    blocks = 2 * seqs
    steps = peers * rows // 2
    z, plane = chan // peers, chan % peers
    block = seq * 2 + z
    me = seq * chans + chan
    count = seqs * chans
    after, prior = (me + 1) % count, (me + count - 1) % count

    def in_plane(p):
        return (seq, z * peers + p)

    def in_column(b):
        return (b // 2, (b % 2) * peers + plane)

    def of_all(i):
        return (i // chans, i % chans)

    barrier = pltpu.get_barrier_semaphore()

    def greet(device):
        pl.semaphore_signal(barrier, inc=1, device_id=device, device_id_type=MESH)

    greet(of_all(prior))

    @pl.loop(1, peers)
    def _(k):
        greet(in_plane((plane + k) % peers))

    @pl.loop(1, blocks)
    def _(k):
        greet(in_column((block + k) % blocks))

    for s in range(3):
        rim_ref[s] = feat_ref[s, rows - 2 : rows, :]
    rates = rates_ref[...]
    modes_ref[z, 0:MODES, :] = rates
    modes_ref[z, MODES : 2 * MODES, :] = mode_gain(rates, residues_ref[...])
    modes_ref[z, 2 * MODES : 2 * MODES + 8, :] = jnp.broadcast_to(skipin_ref[...], (8, HALF))
    one, two = tap_masks(me * rows, doc_ref, rows)

    pl.semaphore_wait(barrier, peers + blocks - 1)

    rim = pltpu.make_async_remote_copy(
        rim_ref, rimin_ref, pair_send.at[0], pair_recv.at[0], device_id=of_all(after), device_id_type=MESH
    )
    rim.start()

    def params(slot):
        return pltpu.make_async_remote_copy(
            modes_ref.at[slot], modes_ref.at[slot], pair_send.at[1], pair_recv.at[1],
            device_id=in_plane_of_other(), device_id_type=MESH,
        )

    def in_plane_of_other():
        return (seq, (1 - z) * peers + plane)

    params(z).start()
    rim.wait_recv()

    def there(p, slot):
        return pltpu.make_async_remote_copy(
            prod_ref.at[p], recv_ref.at[slot], there_send.at[p], there_recv.at[slot],
            device_id=in_plane(p), device_id_type=MESH,
        )

    def make(p):
        for half in range(2):
            value = featurize(half * peers + p, one, two, feat_ref, rimin_ref, short_ref, gate_ref)
            prod_ref[p, :, half * HALF : (half + 1) * HALF] = value

    @pl.loop(1, peers)
    def _(k):
        p = (plane + k) % peers
        make(p)
        there(p, plane).start()

    make(plane)
    recv_ref[plane] = prod_ref[plane]
    spread(plane, recv_ref, u_ref)
    params(1 - z).wait_recv()
    scatter_params(modes_ref, rate_ref, gain_ref, skip_ref)
    for m in range(MODES):
        put_rows(fade_ref, m, jnp.exp(-2.0 * steps * rate_ref[m * 8 : m * 8 + 4, :]))

    @pl.loop(1, peers)
    def _(k):
        p = (plane + peers - k) % peers
        there(plane, p).wait_recv()
        spread(p, recv_ref, u_ref)

    local_states(u_ref, rate_ref, end_ref, steps)
    block_states(end_ref, rate_ref, state_ref, steps)

    def state_copy(b, slot):
        return pltpu.make_async_remote_copy(
            state_ref.at[b], states_ref.at[slot], ring_send.at[b], ring_recv.at[slot],
            device_id=in_column(b), device_id_type=MESH,
        )

    def carry_copy(b, slot):
        return pltpu.make_async_remote_copy(
            carries_ref.at[b], carry_ref.at[slot], ring_send.at[blocks + b], ring_recv.at[blocks + slot],
            device_id=in_column(b), device_id_type=MESH,
        )

    @pl.loop(1, blocks)
    def _(k):
        state_copy((block + k) % blocks, block).start()

    states_ref[block] = state_ref[block]

    zero = (jnp.zeros((8, LANES), jnp.float32),) * MODES
    x = local_outputs(zero, 0, steps // 2, u_ref, rate_ref, gain_ref, skip_ref, y_ref, steps)

    @pl.loop(1, blocks)
    def _(k):
        state_copy(block, (block + k) % blocks).wait_recv()

    fade = fade_ref[block]

    def chain(b, carry):
        carries_ref[b] = carry
        return fade * carry + states_ref[b]

    lax.fori_loop(0, blocks, chain, jnp.zeros_like(fade))

    @pl.loop(1, blocks)
    def _(k):
        carry_copy((block + k) % blocks, block).start()

    carry_ref[block] = carries_ref[block]
    local_outputs(x, steps // 2, steps, u_ref, rate_ref, gain_ref, skip_ref, y_ref, steps)

    @pl.loop(1, blocks)
    def _(k):
        carry_copy(block, (block + k) % blocks).wait_recv()

    carried(end_ref, carry_ref, rate_ref, gain_ref, base_ref, steps)

    def back(p, slot):
        return pltpu.make_async_remote_copy(
            mixed_ref.at[p], back_ref.at[slot], back_send.at[p], back_recv.at[slot],
            device_id=in_plane(p), device_id_type=MESH,
        )

    @pl.loop(0, peers // 2)
    def _(k):
        i = (plane + k) % (peers // 2)
        add_carried(i, rows, base_ref, rate_ref, y_ref, steps)
        for h in range(2):
            p = h * (peers // 2) + i
            gathered(y_ref, mixed_ref, p, h, i * rows, rows, steps)

            @pl.when(p != plane)
            def _():
                back(p, plane).start()

    back_ref[plane] = mixed_ref[plane]

    def finish(p):
        for half in range(2):
            cols = pl.ds(pl.multiple_of((half * peers + p) * HALF, HALF), HALF)
            value = back_ref[p, :, half * HALF : (half + 1) * HALF].astype(jnp.float32)
            out_ref[:, cols] = (gate_ref[:, cols].astype(jnp.float32) * value).astype(jnp.bfloat16)

    finish(plane)

    @pl.loop(1, peers)
    def _(k):
        p = (plane + k) % peers
        back(plane, p).wait_recv()
        finish(p)

    rim.wait_send()
    params(z).wait_send()

    @pl.loop(1, peers)
    def _(k):
        p = (plane + k) % peers
        there(p, plane).wait_send()
        back(p, plane).wait_send()

    @pl.loop(1, blocks)
    def _(k):
        b = (block + k) % blocks
        state_copy(b, block).wait_send()
        carry_copy(b, block).wait_send()


def per_device(features, short_weights, doc_lengths, residues, rates, skip):
    blocks = 2 * lax.axis_size("seq")
    peers = lax.axis_size("chan") // 2
    rows, width = features.shape[1:]
    wide = pltpu.VMEM((peers * rows * QUADS, LANES), jnp.float32)
    table = pltpu.VMEM((8 * MODES, LANES), jnp.float32)
    rim = pltpu.VMEM((3, 2, width), jnp.bfloat16)
    moved = pltpu.VMEM((peers, rows, 2 * HALF), jnp.bfloat16)
    slices = pltpu.VMEM((blocks, MODES * QUADS // blocks, LANES), jnp.float32)
    dma = pltpu.SemaphoreType.DMA
    return pl.pallas_call(
        kernel,
        out_shape=jax.ShapeDtypeStruct((rows, width), jnp.bfloat16),
        in_specs=[VMEM] * 6,
        out_specs=VMEM,
        scratch_shapes=[
            rim, rim,
            pltpu.VMEM((2, 2 * MODES + 8, HALF), jnp.float32),
            pltpu.VMEM((rows, width), jnp.bfloat16),
            moved, moved, wide, wide, moved, moved,
            table, table, pltpu.VMEM((8, LANES), jnp.float32), table, table,
            slices, slices, slices, slices, slices,
            dma((2,)), dma((2,)), dma((peers,)), dma((peers,)), dma((peers,)), dma((peers,)),
            dma((2 * blocks,)), dma((2 * blocks,)),
        ],
        compiler_params=pltpu.CompilerParams(
            collective_id=0, has_side_effects=True, vmem_limit_bytes=40 * 2**20
        ),
    )(doc_lengths[None, :], features, short_weights, residues, rates, skip[None, :])


def solution(mesh):
    placed = (P(None, ("seq", "chan"), None), P(), P(), P(None, "chan"), P(None, "chan"), P("chan"))
    return jax.shard_map(
        per_device, mesh=mesh, in_specs=placed, out_specs=P(("seq", "chan"), None), check_vma=False
    )
```

time: 344 us -> 81 us (0.24)
  waiting for transfers between devices: 276 us -> 0 us
  Pallas kernels: 11.1 us -> 74.7 us
  starting transfers between devices: 21.4 us -> 0 us
  between operations: 13.5 us -> 0.02 us
  blocking collectives: 13.1 us -> 0 us
    all_gather x1 -> x0, waiting for transfers between devices: 254 us -> none  [per_device(): states = lax.all_gather(state, ('seq', 'chan'), axis_index_groups=column)]
    pallas_call x3 -> x1, Pallas kernels: 11.1 us -> 74.7 us  [per_device(): pl.pallas_call(kernel, out_shape=jax.ShapeDtypeStruct((rows, width), jnp....]
    ppermute x2 -> x0, waiting for transfers between devices: 21.3 us -> none  [the longest x1 19.9 us: per_device(): lax.ppermute(features[:, rows - 2:, :], ('seq', 'chan'), [(i, (i + 1) % c...]
    ppermute x2 -> x0, starting transfers between devices: 17.8 us -> none  [the longest x1 13.9 us: per_device(): lax.ppermute(mine, 'chan', [(i, (i + peers) % chans) for i in range(chans)])]
    all_to_all x1 -> x0, blocking collectives: 13.1 us -> none  [per_device(): lax.all_to_all(mixed, 'chan', 0, 0, axis_index_groups=plane, tiled=True)]
    all_to_all x1 -> x0, starting transfers between devices: 3.57 us -> none  [per_device(): lax.all_to_all(product, 'chan', 0, 0, axis_index_groups=plane, tiled=True)]
  transfers between devices with their start and end apart: 4 -> 0, of which waited for: 3 -> 0; matrix products, arithmetic and copies ran while one was open for 0% -> 0% of each run, Pallas kernels for 0% -> 0%
where the time goes in v2:
time: 81 us; the launch traced here: 80.7 us
  Pallas kernels  74.7 us (92%)
  local copies, waits for them, and re-layouts  5.97 us (7%)
    pallas_call x1, Pallas kernels, per_device(): pl.pallas_call(kernel, out_shape=jax.ShapeDtypeStruct((rows, width), jnp....  74.7 us
    unnamed x13, local copies, waits for them, and re-layouts  5.97 us

profile of v2, /device:TPU:1, one launch (start us, length us, event | category | flops | bytes accessed | tf_op | source)
XLA Modules:
  0.0 80.7 jit_solution(14797843056931384675)
XLA Ops:
  0.0 0.0 copy-start
  0.0 1.4 %copy-done = bf16[3,32,8192]{2,1,0:T(8,128)(2,1)S(1)} copy-done((bf16[3,32,8192]{2,1,0:T(8,128)(2,1)S(1)}, bf16[3,32,8192]{2,1,0:T(8,128)(2,1)}, u32[]{:S(2)}) %copy-start) | copy-done | bytes 1572888
  1.4 0.0 copy-start.1
  1.4 1.0 %copy-done.1 = f32[3,3,8192]{2,1,0:T(4,128)S(1)} copy-done((f32[3,3,8192]{2,1,0:T(4,128)S(1)}, f32[3,3,8192]{2,1,0:T(4,128)}, u32[]{:S(2)}) %copy-start.1) | copy-done | bytes 294936
  2.4 0.0 copy-start.2
  2.4 0.7 copy-done.2
  3.1 0.0 copy-start.3
  3.1 0.7 copy-done.3
  3.8 0.0 copy-start.4
  3.8 0.7 copy-done.4
  4.5 0.0 copy-start.5
  4.5 0.7 copy-done.5
  5.2 74.7 %shard_map.64 = bf16[32,8192]{1,0:T(8,128)(2,1)S(1)} custom-call(s32[1,64]{1,0:T(1,128)S(1)} %bitcast.3, bf16[3,32,8192]{2,1,0:T(8,128)(2,1)S(1)} %copy-done, f32[3,3,8192]{2,1,0:T(4,128)S(1)} %copy-done.1, f32[16,256]{1,0:T(8,128)S(1)} %copy-done.2, f32[16,256]{1,0:T(8,128)S(1)} %copy-done.3, f32[1,256]{1,0:T(1,128)S(1)} %bitcast.2), custom_call_target="tpu_custom_call" | custom-call | tf_op jit(solution)/shard_map/pallas_call | solution.py:392
  79.9 0.8 copy.8
Async XLA Ops:
  0.0 1.4 %copy-start = (bf16[3,32,8192]{2,1,0:T(8,128)(2,1)S(1)}, bf16[3,32,8192]{2,1,0:T(8,128)(2,1)}, u32[]{:S(2)}) copy-start(bf16[3,32,8192]{2,1,0:T(8,128)(2,1)} %feat_ref.1) | copy-start | bytes 4718596
  1.4 1.0 %copy-start.1 = (f32[3,3,8192]{2,1,0:T(4,128)S(1)}, f32[3,3,8192]{2,1,0:T(4,128)}, u32[]{:S(2)}) copy-start(f32[3,3,8192]{2,1,0:T(4,128)} %short_ref.1) | copy-start | bytes 884740
  2.4 0.7 copy-start.2
  3.1 0.7 copy-start.3
  3.8 0.7 copy-start.4
  4.5 0.7 copy-start.5

commit v3 on v2

v3 whole, which is shorter than its diff:
```python
import jax
import jax.numpy as jnp
from jax import lax
from jax.experimental import pallas as pl
from jax.experimental.pallas import tpu as pltpu
from jax.sharding import PartitionSpec as P

MODES = 16
LANES = 128
QUADS = 4
HALF = 256
VMEM = pl.BlockSpec(memory_space=pltpu.VMEM)
MESH = pl.DeviceIdType.MESH


def doc_starts(doc_ref):
    n = doc_ref.shape[1]
    lengths = doc_ref[...].astype(jnp.float32)
    rows = lax.broadcasted_iota(jnp.int32, (n, n), 0)
    cols = lax.broadcasted_iota(jnp.int32, (n, n), 1)
    wide = jnp.broadcast_to(lengths, (n, n))
    column = jnp.sum(jnp.where(rows == cols, wide, 0.0), axis=1, keepdims=True)
    return jnp.sum(jnp.where(rows < cols, column, 0.0), axis=0, keepdims=True)


def tap_masks(first, doc_ref, rows):
    starts = doc_starts(doc_ref)
    n = starts.shape[1]
    index = lax.broadcasted_iota(jnp.int32, (rows, n), 0)
    position = (first + index).astype(jnp.float32)
    here = jnp.max(jnp.where(starts == position, 1.0, 0.0), axis=1, keepdims=True)
    before = jnp.max(jnp.where(starts == position - 1.0, 1.0, 0.0), axis=1, keepdims=True)
    one = jnp.broadcast_to(here, (rows, HALF)) < 0.5
    two = jnp.broadcast_to(here + before, (rows, HALF)) < 0.5
    return one, two


def filtered(x, x1, x2, one, two, short_ref, s, cols):
    return (
        x * short_ref[s, 0:1, cols]
        + jnp.where(one, x1, 0.0) * short_ref[s, 1:2, cols]
        + jnp.where(two, x2, 0.0) * short_ref[s, 2:3, cols]
    )


def form_product(block, one, two, feat_ref, short_ref):
    rows = one.shape[0]
    cols = pl.ds(pl.multiple_of(block * HALF, HALF), HALF)
    streams, ends = [], []
    for s in (1, 2):
        x = feat_ref[s, :, cols].astype(jnp.float32)
        ends.append((x[0:8], x[rows - 8 : rows]))
        streams.append(
            filtered(x, pltpu.roll(x, 1, 0), pltpu.roll(x, 2, 0), one, two, short_ref, s, cols)
        )
    row = lax.broadcasted_iota(jnp.int32, (8, HALF), 0)
    (key_top, key_end), (value_top, value_end) = ends
    lower = jnp.where(row < 6, pltpu.roll(value_end, 6, 0), key_end)
    upper = jnp.where(row < 2, key_top, pltpu.roll(value_top, 2, 0))
    edges = jnp.where(row < 4, upper, lower)
    return (streams[0] * streams[1]).astype(jnp.bfloat16), edges.astype(jnp.bfloat16)


def form_gate(block, one, two, feat_ref, rim_ref, short_ref, gate_ref):
    row = lax.broadcasted_iota(jnp.int32, one.shape, 0)
    cols = pl.ds(pl.multiple_of(block * HALF, HALF), HALF)
    x = feat_ref[0, :, cols].astype(jnp.float32)
    rim = rim_ref[:, cols].astype(jnp.float32)
    x1 = jnp.where(row == 0, rim[1:2], pltpu.roll(x, 1, 0))
    x2 = jnp.where(row == 0, rim[0:1], jnp.where(row == 1, rim[1:2], pltpu.roll(x, 2, 0)))
    gate_ref[:, cols] = filtered(x, x1, x2, one, two, short_ref, 0, cols).astype(jnp.bfloat16)


def repair(first, rows, plane, doc_ref, short_ref, edge_ref, u_ref):
    peers = edge_ref.shape[0] // (8 * QUADS) - 1
    steps = peers * rows // 2
    starts = doc_starts(doc_ref)
    n = starts.shape[1]
    index = lax.broadcasted_iota(jnp.int32, (peers, n), 0)
    position = (first + index * rows).astype(jnp.float32)

    def begins(shift):
        hit = jnp.where(starts == position + shift, 1.0, 0.0)
        return jnp.broadcast_to(jnp.max(hit, axis=1, keepdims=True), (peers, HALF))

    before, here, later = begins(-1.0), begins(0.0), begins(1.0)
    one = (here < 0.5, later < 0.5)
    two = (here + before < 0.5, later + here < 0.5)
    for half in range(2):
        cols = pl.ds(pl.multiple_of((half * peers + plane) * HALF, HALF), HALF)
        lanes = slice(half * HALF, (half + 1) * HALF)

        def edge(slot, r):
            parts = [
                edge_ref[pl.ds((half * 2 + i) * 8 * (peers + 1) + slot * 8 + r, peers, stride=8), :]
                for i in range(HALF // LANES)
            ]
            return jnp.concatenate(parts, axis=1)

        fixed = []
        for s, top, last in ((1, 0, 6), (2, 2, 4)):
            x = [edge(0, last), edge(0, last + 1), edge(1, top), edge(1, top + 1)]
            fixed.append(
                [
                    filtered(x[2 + i], x[1 + i], x[i], one[i], two[i], short_ref, s, cols)
                    for i in range(2)
                ]
            )
        for i in range(2):
            value = (fixed[0][i] * fixed[1][i]).astype(jnp.bfloat16).astype(jnp.float32)
            for h in range(2):
                for j in range(HALF // LANES):
                    q = half * (HALF // LANES) + j
                    at = pl.ds((h * QUADS + q) * steps + i, peers // 2, stride=rows)
                    u_ref[at, :] = value[h * (peers // 2) : (h + 1) * (peers // 2), j * LANES : (j + 1) * LANES]


def mode_gain(rate, residue):
    x = 2.0 * rate
    series = jnp.ones_like(x)
    for n in range(9, 1, -1):
        series = 1.0 - x * (1.0 / n) * series
    return residue * jnp.sqrt(x * series)


def scatter_rates(modes_ref, rate_ref):
    for q in range(QUADS):
        cols = slice((q % 2) * LANES, (q % 2 + 1) * LANES)
        for h in range(2):
            rate_ref[pl.ds(h * QUADS + q, MODES, stride=8), :] = modes_ref[q // 2, 0:MODES, cols]


def scatter_gains(modes_ref, gain_ref, skip_ref):
    for q in range(QUADS):
        cols = slice((q % 2) * LANES, (q % 2 + 1) * LANES)
        for h in range(2):
            at = h * QUADS + q
            gain_ref[pl.ds(at, MODES, stride=8), :] = modes_ref[q // 2, MODES : 2 * MODES, cols]
            skip_ref[at : at + 1, :] = modes_ref[q // 2, 2 * MODES : 2 * MODES + 1, cols]


def spread(p, recv_ref, u_ref):
    peers, rows, _ = recv_ref.shape
    steps = peers * rows // 2
    h = p // (peers // 2)
    t = (p % (peers // 2)) * rows
    for q in range(QUADS):
        at = pl.multiple_of((h * QUADS + q) * steps + t, 32)
        u_ref[pl.ds(at, rows), :] = recv_ref[p, :, q * LANES : (q + 1) * LANES].astype(jnp.float32)


def mode_rows(ref):
    return [ref[m * 8 : m * 8 + 8, :] for m in range(MODES)]


def local_states(u_ref, rate_ref, end_ref, steps):
    decay = [jnp.exp(-x) for x in mode_rows(rate_ref)]

    def step(t, x):
        u = u_ref[pl.ds(t, 8, stride=steps), :]
        return tuple(d * a + u for d, a in zip(decay, x))

    zero = jnp.zeros((8, LANES), jnp.float32)
    x = lax.fori_loop(0, steps, step, (zero,) * MODES, unroll=8)
    for m in range(MODES):
        end_ref[m * 8 : m * 8 + 8, :] = x[m]


def block_states(end_ref, rate_ref, state_ref, steps):
    for m in range(MODES):
        x = end_ref[m * 8 : m * 8 + 8, :]
        rate = rate_ref[m * 8 : m * 8 + 4, :]
        state = jnp.exp(-float(steps) * rate) * x[0:4] + x[4:8]
        put_rows(state_ref, m, state)


def put_rows(ref, m, value):
    height = ref.shape[1]
    if height <= QUADS:
        for i in range(QUADS // height):
            ref[m * (QUADS // height) + i] = value[i * height : (i + 1) * height]
    else:
        each = height // QUADS
        ref[m // each, (m % each) * QUADS : (m % each + 1) * QUADS, :] = value


def get_rows(ref, m):
    height = ref.shape[1]
    if height <= QUADS:
        n = QUADS // height
        return jnp.concatenate([ref[m * n + i] for i in range(n)], axis=0)
    each = height // QUADS
    return ref[m // each, (m % each) * QUADS : (m % each + 1) * QUADS, :]


def local_outputs(x, begin, end, u_ref, rate_ref, gain_ref, skip_ref, y_ref, steps):
    decay = [jnp.exp(-x) for x in mode_rows(rate_ref)]
    gain = mode_rows(gain_ref)
    skip = skip_ref[...]

    def step(t, x):
        u = u_ref[pl.ds(t, 8, stride=steps), :]
        x = tuple(d * a + u for d, a in zip(decay, x))
        y_ref[pl.ds(t, 8, stride=steps), :] = total([g * a for g, a in zip(gain, x)] + [skip * u])
        return x

    return lax.fori_loop(begin, end, step, x, unroll=4)


def total(parts):
    while len(parts) > 1:
        parts = [sum(parts[i : i + 2]) for i in range(0, len(parts), 2)]
    return parts[0]


def carried(end_ref, carry_ref, rate_ref, gain_ref, base_ref, steps):
    for m in range(MODES):
        carry = get_rows(carry_ref, m)
        rate = rate_ref[m * 8 : m * 8 + 4, :]
        later = end_ref[m * 8 : m * 8 + 4, :] + jnp.exp(-float(steps) * rate) * carry
        both = jnp.concatenate([carry, later], axis=0)
        base_ref[m * 8 : m * 8 + 8, :] = gain_ref[m * 8 : m * 8 + 8, :] * both


def add_carried(i, rows, base_ref, rate_ref, y_ref, steps):
    rate = mode_rows(rate_ref)
    decay = [jnp.exp(-x) for x in rate]
    begin = i * rows
    past = begin.astype(jnp.float32)
    state = tuple(a * jnp.exp(-past * r) for a, r in zip(mode_rows(base_ref), rate))

    def step(t, state):
        state = tuple(d * a for d, a in zip(decay, state))
        at = pl.ds(begin + t, 8, stride=steps)
        y_ref[at, :] = y_ref[at, :] + total(list(state))
        return state

    lax.fori_loop(0, rows, step, state, unroll=8)


def gathered(y_ref, out_ref, p, h, t, rows, steps):
    for q in range(QUADS):
        at = pl.multiple_of((h * QUADS + q) * steps + t, 32)
        out_ref[p, :, q * LANES : (q + 1) * LANES] = y_ref[pl.ds(at, rows), :].astype(jnp.bfloat16)


def kernel(
    doc_hbm, feat_hbm, short_hbm, residues_hbm, rates_hbm, skip_hbm,
    out_ref,
    doc_ref, feat_ref, short_ref, residues_ref, rates_ref, skipin_ref,
    rim_ref, rimin_ref, modes_ref, gate_ref, prod_ref, recv_ref, edge_ref, edges_ref, cross_ref, edgewide_ref,
    u_ref, y_ref, mixed_ref, back_ref,
    rate_ref, gain_ref, skip_ref, end_ref, base_ref, state_ref, packed_ref, states_ref, carries_ref, carry_ref, fade_ref,
    load, pair_send, pair_recv, cross_send, there_send, there_recv, edge_send, edge_recv, back_send, back_recv,
    ring_send, ring_recv, near_send, near_recv,
):
    seqs, chans = lax.axis_size("seq"), lax.axis_size("chan")
    seq, chan = lax.axis_index("seq"), lax.axis_index("chan")
    peers, rows, _ = prod_ref.shape
    blocks = 2 * seqs
    owners = state_ref.shape[0]
    steps = peers * rows // 2
    z, plane = chan // peers, chan % peers
    block = seq * 2 + z
    me = seq * chans + chan
    count = seqs * chans
    after, prior = (me + 1) % count, (me + count - 1) % count

    def in_plane(p):
        return (seq, z * peers + p)

    def in_column(b):
        return (b // 2, (b % 2) * peers + plane)

    def of_all(i):
        return (i // chans, i % chans)

    def remote(src, dst, send, recv, device):
        return pltpu.make_async_remote_copy(src, dst, send, recv, device_id=device, device_id_type=MESH)

    barrier = pltpu.get_barrier_semaphore()

    def greet(device):
        pl.semaphore_signal(barrier, inc=1, device_id=device, device_id_type=MESH)

    @pl.loop(1, blocks)
    def _(k):
        greet(in_column((block + k) % blocks))

    behind = (block + blocks - 1) % blocks
    greet((behind // 2, (behind % 2) * peers + peers - 1))
    greet(of_all(prior))

    @pl.loop(1, peers)
    def _(k):
        greet(in_plane((plane + k) % peers))

    pairs = (
        (feat_hbm, feat_ref), (short_hbm, short_ref), (doc_hbm, doc_ref), (rates_hbm, rates_ref),
        (residues_hbm, residues_ref), (skip_hbm, skipin_ref),
    )
    loads = [pltpu.make_async_copy(src, dst, load.at[i]) for i, (src, dst) in enumerate(pairs)]
    for copy in loads:
        copy.start()
    for copy in loads[2:]:
        copy.wait()
    rates = rates_ref[...]
    modes_ref[z, 0:MODES, :] = rates
    modes_ref[z, MODES : 2 * MODES, :] = mode_gain(rates, residues_ref[...])
    modes_ref[z, 2 * MODES : 2 * MODES + 8, :] = jnp.broadcast_to(skipin_ref[...], (8, HALF))
    one, two = tap_masks(me * rows, doc_ref, rows)
    for copy in loads[:2]:
        copy.wait()
    rim_ref[...] = feat_ref[0, rows - 2 : rows, :]

    @pl.loop(0, peers)
    def _(p):
        for half in range(2):
            value, edges = form_product(half * peers + p, one, two, feat_ref, short_ref)
            prod_ref[p, :, half * HALF : (half + 1) * HALF] = value
            edge_ref[p, :, half * HALF : (half + 1) * HALF] = edges

    pl.semaphore_wait(barrier, peers + blocks - 1 + peers * (plane // (peers - 1)))

    partner = (seq, (1 - z) * peers + plane)

    def params(slot, part):
        at = modes_ref.at[slot, pl.ds(0, MODES)] if part == 0 else modes_ref.at[slot, pl.ds(MODES, MODES + 8)]
        return remote(at, at, pair_send.at[part], pair_recv.at[part], partner)

    params(z, 0).start()

    def cross(p):
        ahead = (block + 1) % blocks
        return remote(
            edge_ref.at[p], cross_ref, cross_send.at[p], pair_recv.at[3],
            (ahead // 2, (ahead % 2) * peers + p),
        )

    @pl.when(plane == peers - 1)
    def _():
        @pl.loop(0, peers)
        def _(p):
            cross(p).start()

    def edges_there(p, slot):
        return remote(edge_ref.at[p], edges_ref.at[slot], edge_send.at[p], edge_recv.at[slot], in_plane(p))

    def there(p, slot):
        return remote(prod_ref.at[p], recv_ref.at[slot], there_send.at[p], there_recv.at[slot], in_plane(p))

    @pl.loop(1, peers)
    def _(k):
        p = (plane + k) % peers
        there(p, plane).start()
        edges_there(p, plane).start()

    params(z, 1).start()
    rim = remote(rim_ref, rimin_ref, pair_send.at[2], pair_recv.at[2], of_all(after))
    rim.start()

    def widen(slot, value):
        for q in range(QUADS):
            at = pl.multiple_of((q * (peers + 1) + slot) * 8, 8)
            edgewide_ref[pl.ds(at, 8), :] = value[:, q * LANES : (q + 1) * LANES].astype(jnp.float32)

    def take(p, source, edges):
        spread(p, source, u_ref)
        widen(p + 1, edges[p])

    take(plane, prod_ref, edge_ref)

    @pl.loop(1, peers)
    def _(k):
        p = (plane + peers - k) % peers
        there(plane, p).wait_recv()
        edges_there(plane, p).wait_recv()
        take(p, recv_ref, edges_ref)

    params(1 - z, 0).wait_recv()
    scatter_rates(modes_ref, rate_ref)
    cross(plane).wait_recv()
    widen(0, cross_ref[...])
    repair(block * peers * rows, rows, plane, doc_ref, short_ref, edgewide_ref, u_ref)

    local_states(u_ref, rate_ref, end_ref, steps)
    block_states(end_ref, rate_ref, state_ref, steps)
    packed_ref[...] = state_ref[...].astype(jnp.bfloat16)

    def owned(b):
        return (b // 2) % owners

    def state_copy(b, slot):
        return remote(packed_ref.at[owned(b)], states_ref.at[slot], ring_send.at[b], ring_recv.at[slot], in_column(b))

    @pl.loop(1, blocks)
    def _(k):
        state_copy((block + k) % blocks, block).start()

    states_ref[block] = packed_ref[owned(block)]
    params(1 - z, 1).wait_recv()
    scatter_gains(modes_ref, gain_ref, skip_ref)
    for m in range(MODES):
        put_rows(fade_ref, m, jnp.exp(-2.0 * steps * rate_ref[m * 8 : m * 8 + 4, :]))
    zero = (jnp.zeros((8, LANES), jnp.float32),) * MODES
    local_outputs(zero, 0, steps, u_ref, rate_ref, gain_ref, skip_ref, y_ref, steps)
    rim.wait_recv()

    @pl.loop(0, 2 * peers)
    def _(i):
        form_gate(i, one, two, feat_ref, rimin_ref, short_ref, gate_ref)

    @pl.loop(1, blocks)
    def _(k):
        state_copy(block, (block + k) % blocks).wait_recv()

    fade = fade_ref[owned(block)]

    def chain(b, carry):
        carries_ref[b] = carry
        return fade * carry + states_ref[b].astype(jnp.float32)

    lax.fori_loop(0, blocks, chain, jnp.zeros_like(fade))
    group = seq // owners * owners

    def near(j):
        return group + (owned(block) + j) % owners

    def carry_copy(to, slot):
        return remote(
            carries_ref.at[to * 2 + z], carry_ref.at[slot], near_send.at[to % owners], near_recv.at[slot],
            (to, chan),
        )

    @pl.loop(1, owners)
    def _(j):
        carry_copy(near(j), owned(block)).start()

    carry_ref[owned(block)] = carries_ref[block]

    @pl.loop(1, owners)
    def _(j):
        carry_copy(seq, near(j) % owners).wait_recv()

    carried(end_ref, carry_ref, rate_ref, gain_ref, base_ref, steps)

    def back(p, slot):
        return remote(mixed_ref.at[p], back_ref.at[slot], back_send.at[p], back_recv.at[slot], in_plane(p))

    @pl.loop(0, peers // 2)
    def _(k):
        i = (plane + k) % (peers // 2)
        add_carried(i, rows, base_ref, rate_ref, y_ref, steps)
        for h in range(2):
            p = h * (peers // 2) + i
            gathered(y_ref, mixed_ref, p, h, i * rows, rows, steps)

            @pl.when(p != plane)
            def _():
                back(p, plane).start()

    def finish(p, source):
        for half in range(2):
            cols = pl.ds(pl.multiple_of((half * peers + p) * HALF, HALF), HALF)
            value = source[p, :, half * HALF : (half + 1) * HALF].astype(jnp.float32)
            out_ref[:, cols] = (gate_ref[:, cols].astype(jnp.float32) * value).astype(jnp.bfloat16)

    finish(plane, mixed_ref)

    @pl.loop(1, peers)
    def _(k):
        p = (plane + k) % peers
        back(plane, p).wait_recv()
        finish(p, back_ref)

    rim.wait_send()
    params(z, 0).wait_send()
    params(z, 1).wait_send()

    @pl.when(plane == peers - 1)
    def _():
        @pl.loop(0, peers)
        def _(p):
            cross(p).wait_send()

    @pl.loop(1, peers)
    def _(k):
        p = (plane + k) % peers
        there(p, plane).wait_send()
        edges_there(p, plane).wait_send()
        back(p, plane).wait_send()

    @pl.loop(1, blocks)
    def _(k):
        state_copy((block + k) % blocks, block).wait_send()

    @pl.loop(1, owners)
    def _(j):
        carry_copy(near(j), owned(block)).wait_send()


def per_device(features, short_weights, doc_lengths, residues, rates, skip):
    seqs = lax.axis_size("seq")
    blocks = 2 * seqs
    owners = min(8, seqs)
    peers = lax.axis_size("chan") // 2
    rows, width = features.shape[1:]
    bf16, f32 = jnp.bfloat16, jnp.float32
    vmem = pltpu.VMEM
    operands = (doc_lengths[None, :], features, short_weights, residues, rates, skip[None, :])
    wide = vmem((peers * rows * QUADS, LANES), f32)
    table = vmem((8 * MODES, LANES), f32)
    rim = vmem((2, width), bf16)
    moved = vmem((peers, rows, 2 * HALF), bf16)
    edges = vmem((peers, 8, 2 * HALF), bf16)
    height = MODES * QUADS // owners
    owned = vmem((owners, height, LANES), f32)
    dma = lambda *n: pltpu.SemaphoreType.DMA(n)
    return pl.pallas_call(
        kernel,
        out_shape=jax.ShapeDtypeStruct((rows, width), bf16),
        in_specs=[pl.BlockSpec(memory_space=pl.ANY)] * 6,
        out_specs=VMEM,
        scratch_shapes=[vmem(x.shape, x.dtype) for x in operands]
        + [
            rim, rim,
            vmem((2, 2 * MODES + 8, HALF), f32),
            vmem((rows, width), bf16),
            moved, moved, edges, edges, vmem((8, 2 * HALF), bf16), vmem((8 * QUADS * (peers + 1), LANES), f32),
            wide, wide, moved, moved,
            table, table, vmem((8, LANES), f32), table, table,
            owned, vmem((owners, height, LANES), bf16), vmem((blocks, height, LANES), bf16),
            vmem((blocks, height, LANES), f32), owned, owned,
            dma(6), dma(3), dma(4), dma(peers), dma(peers), dma(peers), dma(peers), dma(peers), dma(peers), dma(peers),
            dma(blocks), dma(blocks), dma(owners), dma(owners),
        ],
        compiler_params=pltpu.CompilerParams(
            collective_id=0, has_side_effects=True, vmem_limit_bytes=58 * 2**20
        ),
    )(*operands)


def solution(mesh):
    placed = (P(None, ("seq", "chan"), None), P(), P(), P(None, "chan"), P(None, "chan"), P("chan"))
    return jax.shard_map(
        per_device, mesh=mesh, in_specs=placed, out_specs=P(("seq", "chan"), None), check_vma=False
    )
```

time: 81 us -> 70.8 us (0.87)
  Pallas kernels: 74.7 us -> 68.7 us
  local copies, waits for them, and re-layouts: 5.97 us -> 1.87 us
    pallas_call x1, Pallas kernels: 74.7 us -> 68.7 us  [per_device(): pl.pallas_call(kernel, out_shape=jax.ShapeDtypeStruct((rows, width), bf16...]
    unnamed x13 -> x1, local copies, waits for them, and re-layouts: 5.97 us -> 1.87 us
where the time goes in v3:
time: 70.8 us; the launch traced here: 70.6 us
  Pallas kernels  68.7 us (97%)
  local copies, waits for them, and re-layouts  1.87 us (3%)
    pallas_call x1, Pallas kernels, per_device(): pl.pallas_call(kernel, out_shape=jax.ShapeDtypeStruct((rows, width), bf16...  68.7 us
    unnamed x1, local copies, waits for them, and re-layouts  1.87 us

profile of v3, /device:TPU:1, one launch (start us, length us, event | category | flops | bytes accessed | tf_op | source)
XLA Modules:
  0.0 70.6 jit_solution(8120196768167230998)
XLA Ops:
  0.0 68.7 %shard_map.64 = bf16[32,8192]{1,0:T(8,128)(2,1)} custom-call(s32[1,64]{1,0:T(1,128)} %bitcast.3, bf16[3,32,8192]{2,1,0:T(8,128)(2,1)} %feat_hbm.1, f32[3,3,8192]{2,1,0:T(4,128)} %short_hbm.1, f32[16,256]{1,0:T(8,128)} %residues_hbm.1, f32[16,256]{1,0:T(8,128)} %rates_hbm.1, f32[1,256]{1,0:T(1,128)} %bitcast.2), custom_call_target="tpu_custom_call" | custom-call | tf_op jit(solution)/shard_map/pallas_call | solution.py:519
  68.7 1.9 %copy.8 = bf16[32,8192]{1,0:T(8,128)(2,1)} copy(bf16[32,8192]{1,0:T(8,128)(2,1)} %shard_map.64) | data formatting | bytes 1048576

commit v4 on v3

--- a/solution.py
+++ b/solution.py
@@ -287,8 +287,6 @@
     def _(k):
         greet(in_column((block + k) % blocks))
 
-    behind = (block + blocks - 1) % blocks
-    greet((behind // 2, (behind % 2) * peers + peers - 1))
     greet(of_all(prior))
 
     @pl.loop(1, peers)
@@ -320,7 +318,7 @@
             prod_ref[p, :, half * HALF : (half + 1) * HALF] = value
             edge_ref[p, :, half * HALF : (half + 1) * HALF] = edges
 
-    pl.semaphore_wait(barrier, peers + blocks - 1 + peers * (plane // (peers - 1)))
+    pl.semaphore_wait(barrier, peers + blocks - 1)
 
     partner = (seq, (1 - z) * peers + plane)
 
@@ -329,19 +327,8 @@
         return remote(at, at, pair_send.at[part], pair_recv.at[part], partner)
 
     params(z, 0).start()
-
-    def cross(p):
-        ahead = (block + 1) % blocks
-        return remote(
-            edge_ref.at[p], cross_ref, cross_send.at[p], pair_recv.at[3],
-            (ahead // 2, (ahead % 2) * peers + p),
-        )
-
-    @pl.when(plane == peers - 1)
-    def _():
-        @pl.loop(0, peers)
-        def _(p):
-            cross(p).start()
+    rim = remote(rim_ref, rimin_ref, pair_send.at[2], pair_recv.at[2], of_all(after))
+    rim.start()
 
     def edges_there(p, slot):
         return remote(edge_ref.at[p], edges_ref.at[slot], edge_send.at[p], edge_recv.at[slot], in_plane(p))
@@ -352,34 +339,50 @@
     @pl.loop(1, peers)
     def _(k):
         p = (plane + k) % peers
-        there(p, plane).start()
         edges_there(p, plane).start()
 
+    @pl.loop(1, peers)
+    def _(k):
+        there((plane + k) % peers, plane).start()
+
     params(z, 1).start()
-    rim = remote(rim_ref, rimin_ref, pair_send.at[2], pair_recv.at[2], of_all(after))
-    rim.start()
 
     def widen(slot, value):
         for q in range(QUADS):
             at = pl.multiple_of((q * (peers + 1) + slot) * 8, 8)
             edgewide_ref[pl.ds(at, 8), :] = value[:, q * LANES : (q + 1) * LANES].astype(jnp.float32)
 
-    def take(p, source, edges):
+    def take(p, source):
         spread(p, source, u_ref)
-        widen(p + 1, edges[p])
-
-    take(plane, prod_ref, edge_ref)
+
+    edges_ref[plane] = edge_ref[plane]
+    take(plane, prod_ref)
+
+    @pl.loop(1, peers)
+    def _(k):
+        p = (plane + peers - k) % peers
+        edges_there(plane, p).wait_recv()
+
+    ahead = (block + 1) % blocks
+
+    def cross():
+        return remote(edges_ref.at[peers - 1], cross_ref, cross_send, pair_recv.at[3], in_column(ahead))
+
+    cross().start()
+
+    @pl.loop(0, peers)
+    def _(p):
+        widen(p + 1, edges_ref[p])
 
     @pl.loop(1, peers)
     def _(k):
         p = (plane + peers - k) % peers
         there(plane, p).wait_recv()
-        edges_there(plane, p).wait_recv()
-        take(p, recv_ref, edges_ref)
+        take(p, recv_ref)
 
     params(1 - z, 0).wait_recv()
     scatter_rates(modes_ref, rate_ref)
-    cross(plane).wait_recv()
+    cross().wait_recv()
     widen(0, cross_ref[...])
     repair(block * peers * rows, rows, plane, doc_ref, short_ref, edgewide_ref, u_ref)
 
@@ -477,11 +480,7 @@
     params(z, 0).wait_send()
     params(z, 1).wait_send()
 
-    @pl.when(plane == peers - 1)
-    def _():
-        @pl.loop(0, peers)
-        def _(p):
-            cross(p).wait_send()
+    cross().wait_send()
 
     @pl.loop(1, peers)
     def _(k):
@@ -531,7 +530,7 @@
             table, table, vmem((8, LANES), f32), table, table,
             owned, vmem((owners, height, LANES), bf16), vmem((blocks, height, LANES), bf16),
             vmem((blocks, height, LANES), f32), owned, owned,
-            dma(6), dma(3), dma(4), dma(peers), dma(peers), dma(peers), dma(peers), dma(peers), dma(peers), dma(peers),
+            dma(6), dma(3), dma(4), pltpu.SemaphoreType.DMA, dma(peers), dma(peers), dma(peers), dma(peers), dma(peers), dma(peers),
             dma(blocks), dma(blocks), dma(owners), dma(owners),
         ],
         compiler_params=pltpu.CompilerParams(

time: 70.8 us -> 59.2 us (0.84)
  Pallas kernels: 68.7 us -> 57.1 us
    pallas_call x1, Pallas kernels: 68.7 us -> 57.1 us  [per_device(): pl.pallas_call(kernel, out_shape=jax.ShapeDtypeStruct((rows, width), bf16...]
where the time goes in v4:
time: 59.2 us; the launch traced here: 59 us
  Pallas kernels  57.1 us (96%)
  local copies, waits for them, and re-layouts  1.87 us (3%)
    pallas_call x1, Pallas kernels, per_device(): pl.pallas_call(kernel, out_shape=jax.ShapeDtypeStruct((rows, width), bf16...  57.1 us
    unnamed x1, local copies, waits for them, and re-layouts  1.87 us

profile of v4, /device:TPU:1, one launch (start us, length us, event | category | flops | bytes accessed | tf_op | source)
XLA Modules:
  0.0 59.0 jit_solution(10100499906072969565)
XLA Ops:
  0.0 57.1 %shard_map.64 = bf16[32,8192]{1,0:T(8,128)(2,1)} custom-call(s32[1,64]{1,0:T(1,128)} %bitcast.3, bf16[3,32,8192]{2,1,0:T(8,128)(2,1)} %feat_hbm.1, f32[3,3,8192]{2,1,0:T(4,128)} %short_hbm.1, f32[16,256]{1,0:T(8,128)} %residues_hbm.1, f32[16,256]{1,0:T(8,128)} %rates_hbm.1, f32[1,256]{1,0:T(1,128)} %bitcast.2), custom_call_target="tpu_custom_call" | custom-call | tf_op jit(solution)/shard_map/pallas_call | solution.py:518
  57.2 1.9 %copy.8 = bf16[32,8192]{1,0:T(8,128)(2,1)} copy(bf16[32,8192]{1,0:T(8,128)(2,1)} %shard_map.64) | data formatting | bytes 1048576

commit v5 on v4

--- a/solution.py
+++ b/solution.py
@@ -44,31 +44,48 @@
 
 
 def form_product(block, one, two, feat_ref, short_ref):
-    rows = one.shape[0]
     cols = pl.ds(pl.multiple_of(block * HALF, HALF), HALF)
-    streams, ends = [], []
+    streams = []
     for s in (1, 2):
         x = feat_ref[s, :, cols].astype(jnp.float32)
-        ends.append((x[0:8], x[rows - 8 : rows]))
         streams.append(
             filtered(x, pltpu.roll(x, 1, 0), pltpu.roll(x, 2, 0), one, two, short_ref, s, cols)
         )
+    return (streams[0] * streams[1]).astype(jnp.bfloat16)
+
+
+def form_edges(block, feat_ref):
+    rows = feat_ref.shape[1]
+    cols = pl.ds(pl.multiple_of(block * HALF, HALF), HALF)
     row = lax.broadcasted_iota(jnp.int32, (8, HALF), 0)
-    (key_top, key_end), (value_top, value_end) = ends
+    (key_top, key_end), (value_top, value_end) = [
+        (
+            feat_ref[s, 0:16, cols].astype(jnp.float32)[0:8],
+            feat_ref[s, rows - 16 : rows, cols].astype(jnp.float32)[8:16],
+        )
+        for s in (1, 2)
+    ]
     lower = jnp.where(row < 6, pltpu.roll(value_end, 6, 0), key_end)
     upper = jnp.where(row < 2, key_top, pltpu.roll(value_top, 2, 0))
-    edges = jnp.where(row < 4, upper, lower)
-    return (streams[0] * streams[1]).astype(jnp.bfloat16), edges.astype(jnp.bfloat16)
-
-
-def form_gate(block, one, two, feat_ref, rim_ref, short_ref, gate_ref):
-    row = lax.broadcasted_iota(jnp.int32, one.shape, 0)
+    return jnp.where(row < 4, upper, lower).astype(jnp.bfloat16)
+
+
+def form_gate(block, one, two, feat_ref, short_ref, gate_ref):
     cols = pl.ds(pl.multiple_of(block * HALF, HALF), HALF)
     x = feat_ref[0, :, cols].astype(jnp.float32)
+    gate = filtered(x, pltpu.roll(x, 1, 0), pltpu.roll(x, 2, 0), one, two, short_ref, 0, cols)
+    gate_ref[:, cols] = gate.astype(jnp.bfloat16)
+
+
+def repair_gate(block, one, two, feat_ref, rim_ref, short_ref, gate_ref):
+    row = lax.broadcasted_iota(jnp.int32, (16, HALF), 0)
+    cols = pl.ds(pl.multiple_of(block * HALF, HALF), HALF)
+    x = feat_ref[0, 0:16, cols].astype(jnp.float32)
     rim = rim_ref[:, cols].astype(jnp.float32)
     x1 = jnp.where(row == 0, rim[1:2], pltpu.roll(x, 1, 0))
     x2 = jnp.where(row == 0, rim[0:1], jnp.where(row == 1, rim[1:2], pltpu.roll(x, 2, 0)))
-    gate_ref[:, cols] = filtered(x, x1, x2, one, two, short_ref, 0, cols).astype(jnp.bfloat16)
+    gate = filtered(x, x1, x2, one[0:16], two[0:16], short_ref, 0, cols)
+    gate_ref[0:16, cols] = gate.astype(jnp.bfloat16)
 
 
 def repair(first, rows, plane, doc_ref, short_ref, edge_ref, u_ref):
@@ -283,24 +300,26 @@
     def greet(device):
         pl.semaphore_signal(barrier, inc=1, device_id=device, device_id_type=MESH)
 
-    @pl.loop(1, blocks)
-    def _(k):
-        greet(in_column((block + k) % blocks))
-
-    greet(of_all(prior))
-
-    @pl.loop(1, peers)
-    def _(k):
-        greet(in_plane((plane + k) % peers))
-
     pairs = (
-        (feat_hbm, feat_ref), (short_hbm, short_ref), (doc_hbm, doc_ref), (rates_hbm, rates_ref),
-        (residues_hbm, residues_ref), (skip_hbm, skipin_ref),
+        (feat_hbm.at[pl.ds(1, 2)], feat_ref.at[pl.ds(1, 2)]), (short_hbm, short_ref),
+        (doc_hbm, doc_ref), (rates_hbm, rates_ref), (residues_hbm, residues_ref), (skip_hbm, skipin_ref),
+        (feat_hbm.at[0], feat_ref.at[0]),
     )
     loads = [pltpu.make_async_copy(src, dst, load.at[i]) for i, (src, dst) in enumerate(pairs)]
     for copy in loads:
         copy.start()
-    for copy in loads[2:]:
+
+    @pl.loop(1, blocks)
+    def _(k):
+        greet(in_column((block + k) % blocks))
+
+    greet(of_all(prior))
+
+    @pl.loop(1, peers)
+    def _(k):
+        greet(in_plane((plane + k) % peers))
+
+    for copy in loads[2:6]:
         copy.wait()
     rates = rates_ref[...]
     modes_ref[z, 0:MODES, :] = rates
@@ -309,14 +328,22 @@
     one, two = tap_masks(me * rows, doc_ref, rows)
     for copy in loads[:2]:
         copy.wait()
-    rim_ref[...] = feat_ref[0, rows - 2 : rows, :]
 
     @pl.loop(0, peers)
     def _(p):
         for half in range(2):
-            value, edges = form_product(half * peers + p, one, two, feat_ref, short_ref)
+            edge_ref[p, :, half * HALF : (half + 1) * HALF] = form_edges(half * peers + p, feat_ref)
+
+    def make(k):
+        p = (plane + k) % peers
+        for half in range(2):
+            value = form_product(half * peers + p, one, two, feat_ref, short_ref)
             prod_ref[p, :, half * HALF : (half + 1) * HALF] = value
-            edge_ref[p, :, half * HALF : (half + 1) * HALF] = edges
+
+    soon = peers // 2
+    pl.loop(1, soon)(make)
+    loads[6].wait()
+    rim_ref[...] = feat_ref[0, rows - 2 : rows, :]
 
     pl.semaphore_wait(barrier, peers + blocks - 1)
 
@@ -327,58 +354,65 @@
         return remote(at, at, pair_send.at[part], pair_recv.at[part], partner)
 
     params(z, 0).start()
+
+    def edges_there(p, slot):
+        return remote(edge_ref.at[p], edges_ref.at[slot], edge_send.at[p], edge_recv.at[slot], in_plane(p))
+
+    def there(p, slot):
+        return remote(prod_ref.at[p], recv_ref.at[slot], there_send.at[p], there_recv.at[slot], in_plane(p))
+
+    @pl.loop(1, peers)
+    def _(k):
+        p = (plane + k) % peers
+        edges_there(p, plane).start()
+
+    def send(k):
+        there((plane + k) % peers, plane).start()
+
+    early = min(6, soon)
+    pl.loop(1, early)(send)
+    pl.loop(soon, peers + 1)(make)
+    edges_ref[plane] = edge_ref[plane]
+    last = peers - 1
+
+    @pl.when(plane != last)
+    def _():
+        edges_there(plane, last).wait_recv()
+
+    def cross():
+        ahead = in_column((block + 1) % blocks)
+        return remote(edges_ref.at[last], cross_ref, cross_send, pair_recv.at[3], ahead)
+
+    cross().start()
+    pl.loop(early, peers)(send)
     rim = remote(rim_ref, rimin_ref, pair_send.at[2], pair_recv.at[2], of_all(after))
     rim.start()
-
-    def edges_there(p, slot):
-        return remote(edge_ref.at[p], edges_ref.at[slot], edge_send.at[p], edge_recv.at[slot], in_plane(p))
-
-    def there(p, slot):
-        return remote(prod_ref.at[p], recv_ref.at[slot], there_send.at[p], there_recv.at[slot], in_plane(p))
-
-    @pl.loop(1, peers)
-    def _(k):
-        p = (plane + k) % peers
-        edges_there(p, plane).start()
-
-    @pl.loop(1, peers)
-    def _(k):
-        there((plane + k) % peers, plane).start()
-
     params(z, 1).start()
+
+    @pl.loop(0, 2 * peers)
+    def _(i):
+        form_gate(i, one, two, feat_ref, short_ref, gate_ref)
 
     def widen(slot, value):
         for q in range(QUADS):
             at = pl.multiple_of((q * (peers + 1) + slot) * 8, 8)
             edgewide_ref[pl.ds(at, 8), :] = value[:, q * LANES : (q + 1) * LANES].astype(jnp.float32)
 
-    def take(p, source):
-        spread(p, source, u_ref)
-
-    edges_ref[plane] = edge_ref[plane]
-    take(plane, prod_ref)
-
-    @pl.loop(1, peers)
-    def _(k):
-        p = (plane + peers - k) % peers
-        edges_there(plane, p).wait_recv()
-
-    ahead = (block + 1) % blocks
-
-    def cross():
-        return remote(edges_ref.at[peers - 1], cross_ref, cross_send, pair_recv.at[3], in_column(ahead))
-
-    cross().start()
+    spread(plane, prod_ref, u_ref)
 
     @pl.loop(0, peers)
     def _(p):
+        @pl.when((p != last) & (p != plane))
+        def _():
+            edges_there(plane, p).wait_recv()
+
         widen(p + 1, edges_ref[p])
 
     @pl.loop(1, peers)
     def _(k):
         p = (plane + peers - k) % peers
         there(plane, p).wait_recv()
-        take(p, recv_ref)
+        spread(p, recv_ref, u_ref)
 
     params(1 - z, 0).wait_recv()
     scatter_rates(modes_ref, rate_ref)
@@ -407,12 +441,6 @@
         put_rows(fade_ref, m, jnp.exp(-2.0 * steps * rate_ref[m * 8 : m * 8 + 4, :]))
     zero = (jnp.zeros((8, LANES), jnp.float32),) * MODES
     local_outputs(zero, 0, steps, u_ref, rate_ref, gain_ref, skip_ref, y_ref, steps)
-    rim.wait_recv()
-
-    @pl.loop(0, 2 * peers)
-    def _(i):
-        form_gate(i, one, two, feat_ref, rimin_ref, short_ref, gate_ref)
-
     @pl.loop(1, blocks)
     def _(k):
         state_copy(block, (block + k) % blocks).wait_recv()
@@ -440,6 +468,11 @@
         carry_copy(near(j), owned(block)).start()
 
     carry_ref[owned(block)] = carries_ref[block]
+    rim.wait_recv()
+
+    @pl.loop(0, 2 * peers)
+    def _(i):
+        repair_gate(i, one, two, feat_ref, rimin_ref, short_ref, gate_ref)
 
     @pl.loop(1, owners)
     def _(j):
@@ -517,7 +550,7 @@
     dma = lambda *n: pltpu.SemaphoreType.DMA(n)
     return pl.pallas_call(
         kernel,
-        out_shape=jax.ShapeDtypeStruct((rows, width), bf16),
+        out_shape=pltpu.VMEM((rows, width), bf16),
         in_specs=[pl.BlockSpec(memory_space=pl.ANY)] * 6,
         out_specs=VMEM,
         scratch_shapes=[vmem(x.shape, x.dtype) for x in operands]
@@ -530,7 +563,7 @@
             table, table, vmem((8, LANES), f32), table, table,
             owned, vmem((owners, height, LANES), bf16), vmem((blocks, height, LANES), bf16),
             vmem((blocks, height, LANES), f32), owned, owned,
-            dma(6), dma(3), dma(4), pltpu.SemaphoreType.DMA, dma(peers), dma(peers), dma(peers), dma(peers), dma(peers), dma(peers),
+            dma(7), dma(3), dma(4), pltpu.SemaphoreType.DMA, dma(peers), dma(peers), dma(peers), dma(peers), dma(peers), dma(peers),
             dma(blocks), dma(blocks), dma(owners), dma(owners),
         ],
         compiler_params=pltpu.CompilerParams(

time: 59.2 us -> 56.1 us (0.948)
  Pallas kernels: 57.1 us -> 55.1 us
  local copies, waits for them, and re-layouts: 1.87 us -> 0.8 us
    pallas_call x1, Pallas kernels: 57.1 us -> 55.1 us  [per_device(): pl.pallas_call(kernel, out_shape=pltpu.VMEM((rows, width), bf16), in_spec...]
    unnamed x1, local copies, waits for them, and re-layouts: 1.87 us -> 0.8 us
where the time goes in v5:
time: 56.1 us; the launch traced here: 55.9 us
  Pallas kernels  55.1 us (98%)
  local copies, waits for them, and re-layouts  0.8 us (1%)
    pallas_call x1, Pallas kernels, per_device(): pl.pallas_call(kernel, out_shape=pltpu.VMEM((rows, width), bf16), in_spec...  55.1 us

profile of v5, /device:TPU:1, one launch (start us, length us, event | category | flops | bytes accessed | tf_op | source)
XLA Modules:
  0.0 55.9 jit_solution(14414344304750570499)
XLA Ops:
  0.0 55.1 %shard_map.64 = bf16[32,8192]{1,0:T(8,128)(2,1)S(1)} custom-call(s32[1,64]{1,0:T(1,128)} %bitcast.3, bf16[3,32,8192]{2,1,0:T(8,128)(2,1)} %feat_hbm.1, f32[3,3,8192]{2,1,0:T(4,128)} %short_hbm.1, f32[16,256]{1,0:T(8,128)} %residues_hbm.1, f32[16,256]{1,0:T(8,128)} %rates_hbm.1, f32[1,256]{1,0:T(1,128)} %bitcast.2), custom_call_target="tpu_custom_call" | custom-call | tf_op jit(solution)/shard_map/pallas_call | solution.py:551
  55.1 0.8 %copy.8 = bf16[32,8192]{1,0:T(8,128)(2,1)} copy(bf16[32,8192]{1,0:T(8,128)(2,1)S(1)} %shard_map.64) | data formatting | bytes 1048576

commit v6 on v5

--- a/solution.py
+++ b/solution.py
@@ -6,6 +6,7 @@
 from jax.sharding import PartitionSpec as P
 
 MODES = 16
+EDGES = 8
 LANES = 128
 QUADS = 4
 HALF = 256
@@ -157,13 +158,14 @@
 
 
 def spread(p, recv_ref, u_ref):
-    peers, rows, _ = recv_ref.shape
+    peers, height, _ = recv_ref.shape
+    rows = height - EDGES
     steps = peers * rows // 2
     h = p // (peers // 2)
     t = (p % (peers // 2)) * rows
     for q in range(QUADS):
         at = pl.multiple_of((h * QUADS + q) * steps + t, 32)
-        u_ref[pl.ds(at, rows), :] = recv_ref[p, :, q * LANES : (q + 1) * LANES].astype(jnp.float32)
+        u_ref[pl.ds(at, rows), :] = recv_ref[p, 0:rows, q * LANES : (q + 1) * LANES].astype(jnp.float32)
 
 
 def mode_rows(ref):
@@ -181,6 +183,14 @@
     x = lax.fori_loop(0, steps, step, (zero,) * MODES, unroll=8)
     for m in range(MODES):
         end_ref[m * 8 : m * 8 + 8, :] = x[m]
+
+
+def add_first(u_ref, rate_ref, end_ref, steps):
+    half = lax.broadcasted_iota(jnp.int32, (8, LANES), 0) < QUADS
+    first, second = [jnp.where(half, u_ref[pl.ds(i, 8, stride=steps), :], 0.0) for i in range(2)]
+    for m, rate in enumerate(mode_rows(rate_ref)):
+        late = jnp.exp(-float(steps - 1) * rate) * first + jnp.exp(-float(steps - 2) * rate) * second
+        end_ref[m * 8 : m * 8 + 8, :] = end_ref[m * 8 : m * 8 + 8, :] + late
 
 
 def block_states(end_ref, rate_ref, state_ref, steps):
@@ -265,15 +275,15 @@
     doc_hbm, feat_hbm, short_hbm, residues_hbm, rates_hbm, skip_hbm,
     out_ref,
     doc_ref, feat_ref, short_ref, residues_ref, rates_ref, skipin_ref,
-    rim_ref, rimin_ref, modes_ref, gate_ref, prod_ref, recv_ref, edge_ref, edges_ref, cross_ref, edgewide_ref,
+    rim_ref, rimin_ref, modes_ref, gate_ref, prod_ref, recv_ref, edge_ref, final_ref, cross_ref, edgewide_ref,
     u_ref, y_ref, mixed_ref, back_ref,
     rate_ref, gain_ref, skip_ref, end_ref, base_ref, state_ref, packed_ref, states_ref, carries_ref, carry_ref, fade_ref,
-    load, pair_send, pair_recv, cross_send, there_send, there_recv, edge_send, edge_recv, back_send, back_recv,
+    load, pair_send, pair_recv, cross_send, there_send, there_recv, edge_send, back_send, back_recv,
     ring_send, ring_recv, near_send, near_recv,
 ):
     seqs, chans = lax.axis_size("seq"), lax.axis_size("chan")
     seq, chan = lax.axis_index("seq"), lax.axis_index("chan")
-    peers, rows, _ = prod_ref.shape
+    peers, rows = prod_ref.shape[0], feat_ref.shape[1]
     blocks = 2 * seqs
     owners = state_ref.shape[0]
     steps = peers * rows // 2
@@ -332,13 +342,15 @@
     @pl.loop(0, peers)
     def _(p):
         for half in range(2):
-            edge_ref[p, :, half * HALF : (half + 1) * HALF] = form_edges(half * peers + p, feat_ref)
+            edges = form_edges(half * peers + p, feat_ref)
+            edge_ref[p, :, half * HALF : (half + 1) * HALF] = edges
+            prod_ref[p, rows : rows + EDGES, half * HALF : (half + 1) * HALF] = edges
 
     def make(k):
         p = (plane + k) % peers
         for half in range(2):
             value = form_product(half * peers + p, one, two, feat_ref, short_ref)
-            prod_ref[p, :, half * HALF : (half + 1) * HALF] = value
+            prod_ref[p, 0:rows, half * HALF : (half + 1) * HALF] = value
 
     soon = peers // 2
     pl.loop(1, soon)(make)
@@ -355,16 +367,21 @@
 
     params(z, 0).start()
 
-    def edges_there(p, slot):
-        return remote(edge_ref.at[p], edges_ref.at[slot], edge_send.at[p], edge_recv.at[slot], in_plane(p))
+    last = peers - 1
+
+    def edges_there(p):
+        return remote(edge_ref.at[p], final_ref, edge_send.at[p], pair_recv.at[4], in_plane(p))
 
     def there(p, slot):
         return remote(prod_ref.at[p], recv_ref.at[slot], there_send.at[p], there_recv.at[slot], in_plane(p))
 
-    @pl.loop(1, peers)
-    def _(k):
-        p = (plane + k) % peers
-        edges_there(p, plane).start()
+    @pl.when(plane == last)
+    def _():
+        @pl.loop(0, last)
+        def _(p):
+            edges_there(p).start()
+
+        final_ref[...] = edge_ref[last]
 
     def send(k):
         there((plane + k) % peers, plane).start()
@@ -372,19 +389,19 @@
     early = min(6, soon)
     pl.loop(1, early)(send)
     pl.loop(soon, peers + 1)(make)
-    edges_ref[plane] = edge_ref[plane]
-    last = peers - 1
+    middle = max(early, peers - 4)
+    pl.loop(early, middle)(send)
 
     @pl.when(plane != last)
     def _():
-        edges_there(plane, last).wait_recv()
+        edges_there(plane).wait_recv()
 
     def cross():
         ahead = in_column((block + 1) % blocks)
-        return remote(edges_ref.at[last], cross_ref, cross_send, pair_recv.at[3], ahead)
+        return remote(final_ref, cross_ref, cross_send, pair_recv.at[3], ahead)
 
     cross().start()
-    pl.loop(early, peers)(send)
+    pl.loop(middle, peers)(send)
     rim = remote(rim_ref, rimin_ref, pair_send.at[2], pair_recv.at[2], of_all(after))
     rim.start()
     params(z, 1).start()
@@ -398,29 +415,29 @@
             at = pl.multiple_of((q * (peers + 1) + slot) * 8, 8)
             edgewide_ref[pl.ds(at, 8), :] = value[:, q * LANES : (q + 1) * LANES].astype(jnp.float32)
 
-    spread(plane, prod_ref, u_ref)
-
-    @pl.loop(0, peers)
-    def _(p):
-        @pl.when((p != last) & (p != plane))
-        def _():
-            edges_there(plane, p).wait_recv()
-
-        widen(p + 1, edges_ref[p])
+    def take(p, source):
+        spread(p, source, u_ref)
+        widen(p + 1, source[p, rows : rows + EDGES, :])
+
+    take(plane, prod_ref)
 
     @pl.loop(1, peers)
     def _(k):
         p = (plane + peers - k) % peers
         there(plane, p).wait_recv()
-        spread(p, recv_ref, u_ref)
+        take(p, recv_ref)
 
     params(1 - z, 0).wait_recv()
     scatter_rates(modes_ref, rate_ref)
+    widen(0, jnp.zeros_like(cross_ref))
+    repair(block * peers * rows, rows, plane, doc_ref, short_ref, edgewide_ref, u_ref)
+    for q in range(QUADS):
+        u_ref[q * steps : q * steps + 2, :] = jnp.zeros((2, LANES), jnp.float32)
+    local_states(u_ref, rate_ref, end_ref, steps)
     cross().wait_recv()
     widen(0, cross_ref[...])
     repair(block * peers * rows, rows, plane, doc_ref, short_ref, edgewide_ref, u_ref)
-
-    local_states(u_ref, rate_ref, end_ref, steps)
+    add_first(u_ref, rate_ref, end_ref, steps)
     block_states(end_ref, rate_ref, state_ref, steps)
     packed_ref[...] = state_ref[...].astype(jnp.bfloat16)
 
@@ -515,11 +532,16 @@
 
     cross().wait_send()
 
+    @pl.when(plane == last)
+    def _():
+        @pl.loop(0, last)
+        def _(p):
+            edges_there(p).wait_send()
+
     @pl.loop(1, peers)
     def _(k):
         p = (plane + k) % peers
         there(p, plane).wait_send()
-        edges_there(p, plane).wait_send()
         back(p, plane).wait_send()
 
     @pl.loop(1, blocks)
@@ -544,7 +566,9 @@
     table = vmem((8 * MODES, LANES), f32)
     rim = vmem((2, width), bf16)
     moved = vmem((peers, rows, 2 * HALF), bf16)
-    edges = vmem((peers, 8, 2 * HALF), bf16)
+    sent = vmem((peers, rows + EDGES, 2 * HALF), bf16)
+    edges = vmem((peers, EDGES, 2 * HALF), bf16)
+    edge = vmem((EDGES, 2 * HALF), bf16)
     height = MODES * QUADS // owners
     owned = vmem((owners, height, LANES), f32)
     dma = lambda *n: pltpu.SemaphoreType.DMA(n)
@@ -558,12 +582,12 @@
             rim, rim,
             vmem((2, 2 * MODES + 8, HALF), f32),
             vmem((rows, width), bf16),
-            moved, moved, edges, edges, vmem((8, 2 * HALF), bf16), vmem((8 * QUADS * (peers + 1), LANES), f32),
+            sent, sent, edges, edge, edge, vmem((8 * QUADS * (peers + 1), LANES), f32),
             wide, wide, moved, moved,
             table, table, vmem((8, LANES), f32), table, table,
             owned, vmem((owners, height, LANES), bf16), vmem((blocks, height, LANES), bf16),
             vmem((blocks, height, LANES), f32), owned, owned,
-            dma(7), dma(3), dma(4), pltpu.SemaphoreType.DMA, dma(peers), dma(peers), dma(peers), dma(peers), dma(peers), dma(peers),
+            dma(7), dma(3), dma(5), pltpu.SemaphoreType.DMA, dma(peers), dma(peers), dma(peers), dma(peers), dma(peers),
             dma(blocks), dma(blocks), dma(owners), dma(owners),
         ],
         compiler_params=pltpu.CompilerParams(

time: 56.1 us -> 54.6 us (0.973)
  Pallas kernels: 55.1 us -> 53.6 us
    pallas_call x1, Pallas kernels: 55.1 us -> 53.6 us  [per_device(): pl.pallas_call(kernel, out_shape=pltpu.VMEM((rows, width), bf16), in_spec...]
where the time goes in v6:
time: 54.6 us; the launch traced here: 54.4 us
  Pallas kernels  53.6 us (98%)
  local copies, waits for them, and re-layouts  0.8 us (1%)
    pallas_call x1, Pallas kernels, per_device(): pl.pallas_call(kernel, out_shape=pltpu.VMEM((rows, width), bf16), in_spec...  53.6 us

profile of v6, /device:TPU:1, one launch (start us, length us, event | category | flops | bytes accessed | tf_op | source)
XLA Modules:
  0.0 54.4 jit_solution(11398784270920966418)
XLA Ops:
  0.0 53.6 %shard_map.64 = bf16[32,8192]{1,0:T(8,128)(2,1)S(1)} custom-call(s32[1,64]{1,0:T(1,128)} %bitcast.3, bf16[3,32,8192]{2,1,0:T(8,128)(2,1)} %feat_hbm.1, f32[3,3,8192]{2,1,0:T(4,128)} %short_hbm.1, f32[16,256]{1,0:T(8,128)} %residues_hbm.1, f32[16,256]{1,0:T(8,128)} %rates_hbm.1, f32[1,256]{1,0:T(1,128)} %bitcast.2), custom_call_target="tpu_custom_call" | custom-call | tf_op jit(solution)/shard_map/pallas_call | solution.py:575
  53.6 0.8 %copy.8 = bf16[32,8192]{1,0:T(8,128)(2,1)} copy(bf16[32,8192]{1,0:T(8,128)(2,1)S(1)} %shard_map.64) | data formatting | bytes 1048576

commit v7 on v6

--- a/solution.py
+++ b/solution.py
@@ -520,11 +520,14 @@
 
     finish(plane, mixed_ref)
 
-    @pl.loop(1, peers)
-    def _(k):
-        p = (plane + k) % peers
-        back(plane, p).wait_recv()
-        finish(p, back_ref)
+    @pl.loop(0, peers)
+    def _(k):
+        p = (plane + peers - k // 2) % (peers // 2) + k % 2 * (peers // 2)
+
+        @pl.when(p != plane)
+        def _():
+            back(plane, p).wait_recv()
+            finish(p, back_ref)
 
     rim.wait_send()
     params(z, 0).wait_send()

time: 54.6 us -> 54.6 us (level)
  no operation moved by 1% of the time
where the time goes in v7:
time: 54.6 us; the launch traced here: 54.4 us
  Pallas kernels  53.6 us (98%)
  local copies, waits for them, and re-layouts  0.8 us (1%)
    pallas_call x1, Pallas kernels, per_device(): pl.pallas_call(kernel, out_shape=pltpu.VMEM((rows, width), bf16), in_spec...  53.6 us

profile of v7, /device:TPU:1, one launch (start us, length us, event | category | flops | bytes accessed | tf_op | source)
XLA Modules:
  0.0 54.4 jit_solution(8912041264893614202)
XLA Ops:
  0.0 53.6 %shard_map.64 = bf16[32,8192]{1,0:T(8,128)(2,1)S(1)} custom-call(s32[1,64]{1,0:T(1,128)} %bitcast.3, bf16[3,32,8192]{2,1,0:T(8,128)(2,1)} %feat_hbm.1, f32[3,3,8192]{2,1,0:T(4,128)} %short_hbm.1, f32[16,256]{1,0:T(8,128)} %residues_hbm.1, f32[16,256]{1,0:T(8,128)} %rates_hbm.1, f32[1,256]{1,0:T(1,128)} %bitcast.2), custom_call_target="tpu_custom_call" | custom-call | tf_op jit(solution)/shard_map/pallas_call | solution.py:578
  53.6 0.8 %copy.8 = bf16[32,8192]{1,0:T(8,128)(2,1)} copy(bf16[32,8192]{1,0:T(8,128)(2,1)S(1)} %shard_map.64) | data formatting | bytes 1048576
